TPU v7x, 256 devices: a whole 4x4x8 slice. The times are simulated.
256 devices in a mesh: context: 64 (over z, x, y_hi), tensor: 4 (over y_lo, core).
Axes of the slice: x: 4, y: 4 (y_hi: 2, y_lo: 2; y = y_hi * 2 + y_lo), z: 8, core: 2. Of those that a mesh axis runs over, the one named last changes fastest.
Arguments:
- queries: bfloat16 [256, 128, 128], P('tensor'), may hold values from -18 to 18
- prompt_keys: bfloat16 [256, 8, 128], P('tensor'), may hold values from -6 to 6
- prompt_values: bfloat16 [256, 8, 128], P('tensor'), may hold values from -6 to 6
- cache_keys: bfloat16 [131072, 8, 128], P('context', 'tensor'), may hold values from -6 to 6
- cache_values: bfloat16 [131072, 8, 128], P('context', 'tensor'), may hold values from -6 to 6
- cache_lengths: int32 [64], P('context'), may hold values from 1 to 2048, 98304 in all
- offset: int32 [1], replicated, may hold values from 1 to 32767
- prompt_positions: int32 [256], P('tensor'), may hold values from 0 to 510, as said below
Outputs:
- attended: bfloat16 [256, 128, 128], P('context', 'tensor')
Inputs may be any that keep to these rules, and one draw needn't show every extreme that they name: `cache_lengths`: they sum to three quarters of 131072. `prompt_positions`: strictly increasing from 0 to 510, steps of 1 to 3.
All inputs are finite; a program needn't handle non-finite values. No bound on the sum of `cache_lengths` on one device may be relied on, other than what follows from the above.
Results may differ from a plain program's by a relative error of at most 0.0095.
The roundings to bfloat16 on the way count: a program that leaves them out, or rounds other values in their place, can miss the bound.
Values may be sent and summed in bfloat16 or wider, within the bound.
No kernel may reach another device: no remote copies, remote signals or barrier semaphores. Data moves between devices by JAX's collectives and lax.ppermute only.
A program may use at most 128 MiB of HBM per device.

v0:
```python
import math

import jax
import jax.numpy as jnp
from jax import lax
from jax.sharding import PartitionSpec as P


def rotate(values, position):
    width = values.shape[-1]
    half = width // 2
    freq = jnp.exp(jnp.arange(half, dtype=jnp.float32) * (-2.0 * math.log(500000.0) / width))
    angle = position.astype(jnp.float32)[:, None] * freq[None, :]
    cosine = jnp.cos(angle)[:, None, :]
    sine = jnp.sin(angle)[:, None, :]
    wide = values.astype(jnp.float32)
    first = wide[..., :half]
    second = wide[..., half:]
    return jnp.concatenate(
        [first * cosine - second * sine, second * cosine + first * sine], axis=-1
    )


def body(
    queries,
    prompt_keys,
    prompt_values,
    cache_keys,
    cache_values,
    cache_lengths,
    offset,
    prompt_positions,
):
    position = offset[0] + prompt_positions
    turned_q = rotate(queries, position).astype(jnp.bfloat16)
    turned_k = rotate(prompt_keys, position).astype(jnp.bfloat16)
    local_q, local_k, local_v = (
        lax.all_to_all(turned_q, "tensor", split_axis=1, concat_axis=0, tiled=True),
        lax.all_to_all(turned_k, "tensor", split_axis=1, concat_axis=0, tiled=True),
        lax.all_to_all(prompt_values, "tensor", split_axis=1, concat_axis=0, tiled=True),
    )
    all_rows, head_count, head_dim = local_q.shape
    kv_count = local_k.shape[1]
    group = head_count // kv_count
    scale = 1.0 / math.sqrt(head_dim)
    owned_rows = all_rows // lax.axis_size("context")
    first_row = lax.axis_index("context") * owned_rows
    own_keys = lax.dynamic_slice_in_dim(local_k, first_row, owned_rows, 0)
    own_vals = lax.dynamic_slice_in_dim(local_v, first_row, owned_rows, 0)
    cache_rows = cache_keys.shape[0]
    live = jnp.arange(cache_rows, dtype=jnp.int32) < cache_lengths[0]
    key_rows = first_row + jnp.arange(owned_rows, dtype=jnp.int32)

    def partial_value(piece, start):
        count = piece.shape[0]
        grouped = piece.reshape(count, kv_count, group, head_dim)
        cache_scores = (
            jnp.einsum("rkgd,ckd->rkgc", grouped, cache_keys, preferred_element_type=jnp.float32)
            * scale
        )
        own_scores = (
            jnp.einsum("rkgd,jkd->rkgj", grouped, own_keys, preferred_element_type=jnp.float32)
            * scale
        )
        query_rows = start + jnp.arange(count, dtype=jnp.int32)
        visible = (key_rows[None, :] <= query_rows[:, None])[:, None, None, :]
        cache_scores = jnp.where(live, cache_scores, -jnp.inf)
        own_scores = jnp.where(visible, own_scores, -jnp.inf)
        peak = jnp.maximum(cache_scores.max(-1), own_scores.max(-1))
        cache_weights = jnp.where(live, jnp.exp(cache_scores - peak[..., None]), 0.0).astype(
            jnp.bfloat16
        )
        own_weights = jnp.where(visible, jnp.exp(own_scores - peak[..., None]), 0.0).astype(
            jnp.bfloat16
        )
        total = cache_weights.astype(jnp.float32).sum(-1) + own_weights.astype(jnp.float32).sum(-1)
        output = jnp.einsum(
            "rkgc,ckd->rkgd", cache_weights, cache_values, preferred_element_type=jnp.float32
        )
        output = output + jnp.einsum(
            "rkgj,jkd->rkgd", own_weights, own_vals, preferred_element_type=jnp.float32
        )
        return (
            output.reshape(count, head_count, head_dim),
            peak.reshape(count, head_count),
            total.reshape(count, head_count),
        )

    row_block = math.gcd(all_rows, 64)
    block_count = all_rows // row_block
    blocked = local_q.reshape(block_count, row_block, head_count, head_dim)
    starts = jnp.arange(block_count, dtype=jnp.int32) * row_block

    def one_block(items):
        return partial_value(items[0], items[1])

    outputs, peaks, totals = lax.map(one_block, (blocked, starts))
    outputs = outputs.reshape(all_rows, head_count, head_dim)
    peaks = peaks.reshape(all_rows, head_count)
    totals = totals.reshape(all_rows, head_count)
    got_out, got_peak, got_total = (
        lax.all_to_all(outputs, "context", split_axis=0, concat_axis=0, tiled=True),
        lax.all_to_all(peaks, "context", split_axis=0, concat_axis=0, tiled=True),
        lax.all_to_all(totals, "context", split_axis=0, concat_axis=0, tiled=True),
    )
    got_out = got_out.reshape(-1, owned_rows, head_count, head_dim)
    got_peak = got_peak.reshape(-1, owned_rows, head_count)
    got_total = got_total.reshape(-1, owned_rows, head_count)
    best = got_peak.max(0)
    factor = jnp.exp(got_peak - best[None])
    numer = jnp.sum(factor[..., None] * got_out, axis=0)
    denom = jnp.sum(factor * got_total, axis=0)
    return (numer / denom[..., None]).astype(jnp.bfloat16)


def solution(mesh):
    in_specs = (
        P("tensor", None, None),
        P("tensor", None, None),
        P("tensor", None, None),
        P("context", "tensor", None),
        P("context", "tensor", None),
        P("context"),
        P(),
        P("tensor"),
    )
    out_specs = P("context", "tensor", None)
    return jax.shard_map(body, mesh=mesh, in_specs=in_specs, out_specs=out_specs, check_vma=False)
```

profile of v0, /device:TPU:8, one launch (start us, length us, event | category | flops | bytes accessed | tf_op | source)
XLA Modules:
  0.0 294.5 jit_solution(2000112504491179690)
XLA Ops:
  0.7 0.9 copy_convert_fusion.1
  1.6 0.7 add_convert_fusion.2
  2.6 0.7 pad_maximum_fusion.1
  3.4 5.5 %all-to-all-start.1 = ((bf16[64,8,128]{2,0,1:T(8,128)(2,1)}), bf16[64,8,128]{2,0,1:T(8,128)(2,1)S(1)}, u32[]{:S(2)}, u32[]{:S(2)}) async-start(bf16[64,8,128]{2,0,1:T(8,128)(2,1)} %pad_maximum_fusion.1), calls=%async_computation.1 | async-start | bytes 262144 | tf_op jit(solution)/shard_map/all_to_all | solution.py:39
  8.8 2.8 copy_convert_fusion
  11.7 2.8 subtract_convert_fusion
  14.5 0.7 copy.45
  15.1 3.3 %all-to-all-start.2 = ((bf16[64,8,128]{2,0,1:T(8,128)(2,1)}), bf16[64,8,128]{2,0,1:T(8,128)(2,1)S(1)}, u32[]{:S(2)}, u32[]{:S(2)}) async-start(bf16[64,8,128]{2,0,1:T(8,128)(2,1)} %copy.45), calls=%async_computation.2 | async-start | bytes 262144 | tf_op jit(solution)/shard_map/all_to_all | solution.py:40
  18.5 4.1 %pad_maximum_fusion = bf16[64,128,128]{2,0,1:T(8,128)(2,1)} fusion(bf16[64,128,64]{2,0,1:T(8,128)(2,1)} %get-tuple-element.182, bf16[64,128,64]{2,0,1:T(8,128)(2,1)S(1)} %get-tuple-element.181), kind=kLoop, calls=%fused_computation.35 | loop fusion | flops 4194304 | bytes 4194304 | tf_op jit(solution)/shard_map/concatenate | solution.py:19
  22.6 4.1 %all-to-all-start = ((bf16[64,128,128]{2,0,1:T(8,128)(2,1)}), bf16[64,128,128]{2,0,1:T(8,128)(2,1)S(1)}, u32[]{:S(2)}, u32[]{:S(2)}) async-start(bf16[64,128,128]{2,0,1:T(8,128)(2,1)} %pad_maximum_fusion), calls=%async_computation | async-start | bytes 4194304 | tf_op jit(solution)/shard_map/all_to_all | solution.py:38
  26.7 1.4 copy.48
  28.1 2.3 copy.49
  31.5 19.2 %all-to-all-done = bf16[64,128,128]{2,0,1:T(8,128)(2,1)S(1)} async-done(((bf16[64,128,128]{2,0,1:T(8,128)(2,1)}), bf16[64,128,128]{2,0,1:T(8,128)(2,1)S(1)}, u32[]{:S(2)}, u32[]{:S(2)}) %all-to-all-start) | async-done | bytes 2097184 | tf_op jit(solution)/shard_map/all_to_all | solution.py:38
  50.7 99.4 %while.15 = (s32[]{:T(128)}, f32[4,64,32,128]{3,2,1,0:T(8,128)}, f32[4,64,32]{1,2,0:T(8,128)}, f32[4,64,32]{1,2,0:T(8,128)}, bf16[4,64,32,128]{3,1,2,0:T(8,128)(...) while((s32[]{:T(128)}, f32[4,64,32,128]{3,2,1,0:T(8,128)}, ...), condition=%wide.region_5.6_spmd.clone, body=%wide.region_0.5_spmd.clone.sunk | while | flops 2214942976 | bytes 129293008 | solution.py:97
  50.7 1.2 dynamic_slice.24
  52.7 2.0 fusion.29
  54.7 0.7 iota_compare_fusion.2
  55.4 2.7 bitcast_reduce_fusion.2
  58.5 4.3 %convert_reduce_fusion.4 = f32[64,2,16]{2,0,1:T(8,128)S(1)} fusion(f32[64,2,16]{2,0,1:T(8,128)S(1)} %max.20, f32[2,64,16,2048]{3,2,1,0:T(8,128)S(1)} %get-tuple-element.268, pred[2048]{0:T(1024)(128)(4,1)S(1)} %iota_compare_fusion.2), kind=kLoop, calls=%fused_computation.7.clone.1 | loop fusion | flops 29358080 | bytes 16795648 | tf_op jit(solution)/shard_map/while/body/eval_jaxpr/reduce_sum | solution.py:76
  62.8 1.1 copy-done
  63.9 0.7 copy.77
  64.6 1.3 constant_dynamic-update-slice_fusion.6
  66.0 7.8 %fusion.30 = f32[2,64,16,128]{3,2,1,0:T(8,128)S(1)} fusion(bf16[2048,2,128]{2,0,1:T(8,128)(2,1)} %get-tuple-element.308, f32[2,64,16,2048]{3,2,1,0:T(8,128)} %copy-done, f32[64,2,16]{2,0,1:T(8,128)S(1)} %max.20, pred[2048]{0:T(1024)(128)(4,1)S(1)} %iota_compare_fusion.2), kind=kOutput, calls=%fused_computation.14.clone.1 | convolution fusion | flops 1094713344 | bytes 18884608 | tf_op jit(solution)/shard_map/while/body/eval_jaxpr/rkgc,ckd->rkgd/dot_general | solution.py:77
  74.5 1.1 constant_dynamic-update-slice_fusion.5
  75.6 1.2 dynamic_slice.24
  77.6 2.0 fusion.29
  79.6 0.7 iota_compare_fusion.2
  80.3 2.8 bitcast_reduce_fusion.2
  83.4 4.3 %convert_reduce_fusion.4 = f32[64,2,16]{2,0,1:T(8,128)S(1)} fusion(f32[64,2,16]{2,0,1:T(8,128)S(1)} %max.20, f32[2,64,16,2048]{3,2,1,0:T(8,128)S(1)} %get-tuple-element.268, pred[2048]{0:T(1024)(128)(4,1)S(1)} %iota_compare_fusion.2), kind=kLoop, calls=%fused_computation.7.clone.1 | loop fusion | flops 29358080 | bytes 16795648 | tf_op jit(solution)/shard_map/while/body/eval_jaxpr/reduce_sum | solution.py:76
  87.7 1.1 copy-done
  88.8 0.7 copy.77
  89.5 1.3 constant_dynamic-update-slice_fusion.6
  90.8 7.8 %fusion.30 = f32[2,64,16,128]{3,2,1,0:T(8,128)S(1)} fusion(bf16[2048,2,128]{2,0,1:T(8,128)(2,1)} %get-tuple-element.308, f32[2,64,16,2048]{3,2,1,0:T(8,128)} %copy-done, f32[64,2,16]{2,0,1:T(8,128)S(1)} %max.20, pred[2048]{0:T(1024)(128)(4,1)S(1)} %iota_compare_fusion.2), kind=kOutput, calls=%fused_computation.14.clone.1 | convolution fusion | flops 1094713344 | bytes 18884608 | tf_op jit(solution)/shard_map/while/body/eval_jaxpr/rkgc,ckd->rkgd/dot_general | solution.py:77
  99.4 1.1 constant_dynamic-update-slice_fusion.5
  100.5 1.2 dynamic_slice.24
  102.5 2.0 fusion.29
  105.2 2.7 bitcast_reduce_fusion.2
  108.3 4.3 %convert_reduce_fusion.4 = f32[64,2,16]{2,0,1:T(8,128)S(1)} fusion(f32[64,2,16]{2,0,1:T(8,128)S(1)} %max.20, f32[2,64,16,2048]{3,2,1,0:T(8,128)S(1)} %get-tuple-element.268, pred[2048]{0:T(1024)(128)(4,1)S(1)} %iota_compare_fusion.2), kind=kLoop, calls=%fused_computation.7.clone.1 | loop fusion | flops 29358080 | bytes 16795648 | tf_op jit(solution)/shard_map/while/body/eval_jaxpr/reduce_sum | solution.py:76
  112.6 1.1 copy-done
  113.7 0.7 copy.77
  114.4 1.3 constant_dynamic-update-slice_fusion.6
  115.7 7.8 %fusion.30 = f32[2,64,16,128]{3,2,1,0:T(8,128)S(1)} fusion(bf16[2048,2,128]{2,0,1:T(8,128)(2,1)} %get-tuple-element.308, f32[2,64,16,2048]{3,2,1,0:T(8,128)} %copy-done, f32[64,2,16]{2,0,1:T(8,128)S(1)} %max.20, pred[2048]{0:T(1024)(128)(4,1)S(1)} %iota_compare_fusion.2), kind=kOutput, calls=%fused_computation.14.clone.1 | convolution fusion | flops 1094713344 | bytes 18884608 | tf_op jit(solution)/shard_map/while/body/eval_jaxpr/rkgc,ckd->rkgd/dot_general | solution.py:77
  124.3 1.1 constant_dynamic-update-slice_fusion.5
  125.3 1.2 dynamic_slice.24
  127.3 2.0 fusion.29
  130.0 2.8 bitcast_reduce_fusion.2
  133.1 4.3 %convert_reduce_fusion.4 = f32[64,2,16]{2,0,1:T(8,128)S(1)} fusion(f32[64,2,16]{2,0,1:T(8,128)S(1)} %max.20, f32[2,64,16,2048]{3,2,1,0:T(8,128)S(1)} %get-tuple-element.268, pred[2048]{0:T(1024)(128)(4,1)S(1)} %iota_compare_fusion.2), kind=kLoop, calls=%fused_computation.7.clone.1 | loop fusion | flops 29358080 | bytes 16795648 | tf_op jit(solution)/shard_map/while/body/eval_jaxpr/reduce_sum | solution.py:76
  137.4 1.1 copy-done
  138.5 0.7 copy.77
  139.2 1.3 constant_dynamic-update-slice_fusion.6
  140.6 7.8 %fusion.30 = f32[2,64,16,128]{3,2,1,0:T(8,128)S(1)} fusion(bf16[2048,2,128]{2,0,1:T(8,128)(2,1)} %get-tuple-element.308, f32[2,64,16,2048]{3,2,1,0:T(8,128)} %copy-done, f32[64,2,16]{2,0,1:T(8,128)S(1)} %max.20, pred[2048]{0:T(1024)(128)(4,1)S(1)} %iota_compare_fusion.2), kind=kOutput, calls=%fused_computation.14.clone.1 | convolution fusion | flops 1094713344 | bytes 18884608 | tf_op jit(solution)/shard_map/while/body/eval_jaxpr/rkgc,ckd->rkgd/dot_general | solution.py:77
  149.1 1.1 constant_dynamic-update-slice_fusion.5
  150.2 0.9 copy.50
  151.1 0.8 reshape.162
  151.9 12.2 %all-to-all-start.3 = ((f32[64,1,128]{2,1,0:T(1,128)}), f32[64,1,128]{2,1,0:T(1,128)S(1)}, u32[]{:S(2)}, u32[]{:S(2)}) async-start(f32[64,1,128]{2,1,0:T(1,128)} %reshape.162), calls=%async_computation.3 | async-start | bytes 65536 | tf_op jit(solution)/shard_map/all_to_all | solution.py:103
  164.1 0.9 copy.51
  165.2 10.8 %all-to-all-done.3 = f32[64,1,128]{2,1,0:T(1,128)S(1)} async-done(((f32[64,1,128]{2,1,0:T(1,128)}), f32[64,1,128]{2,1,0:T(1,128)S(1)}, u32[]{:S(2)}, u32[]{:S(2)}) %all-to-all-start.3) | async-done | bytes 32800 | tf_op jit(solution)/shard_map/all_to_all | solution.py:103
  176.0 15.8 %all_to_all.74 = f32[64,1,128]{2,1,0:T(1,128)S(1)} all-to-all(f32[64,1,128]{2,1,0:T(1,128)S(1)} %reshape.164), channel_id=1, replica_groups=mesh['context'=64,'tensor'=4] {'context'}, dimensions={0} | all-to-all | bytes 65536 | tf_op jit(solution)/shard_map/all_to_all | solution.py:104
  191.8 5.7 %all-to-all-start.4 = ((f32[256,32,128]{2,1,0:T(8,128)}), f32[256,32,128]{2,1,0:T(8,128)}, u32[]{:S(2)}, u32[]{:S(2)}) async-start(f32[256,32,128]{2,1,0:T(8,128)} %bitcast.12), calls=%async_computation.4 | async-start | bytes 8388608 | tf_op jit(solution)/shard_map/all_to_all | solution.py:102
  197.9 0.7 reduce.2
  198.8 0.7 reduce.1
  199.8 91.2 %all-to-all-done.4 = f32[256,32,128]{2,1,0:T(8,128)} async-done(((f32[256,32,128]{2,1,0:T(8,128)}), f32[256,32,128]{2,1,0:T(8,128)}, u32[]{:S(2)}, u32[]{:S(2)}) %all-to-all-start.4) | async-done | bytes 4194336 | tf_op jit(solution)/shard_map/all_to_all | solution.py:102
  291.0 2.8 multiply_reduce_fusion
  293.8 0.7 divide_convert_fusion
  (66 shorter events, 11.3 us)
Async XLA Ops:
  3.4 11.8 %all-to-all-start.1 = ((bf16[64,8,128]{2,0,1:T(8,128)(2,1)}), bf16[64,8,128]{2,0,1:T(8,128)(2,1)S(1)}, u32[]{:S(2)}, u32[]{:S(2)}) async-start(bf16[64,8,128]{2,0,1:T(8,128)(2,1)} %pad_maximum_fusion.1), calls=%async_computation.1 | async-start | bytes 262144 | tf_op jit(solution)/shard_map/all_to_all | solution.py:39
  11.7 2.8 copy-start.1
  15.1 7.4 %all-to-all-start.2 = ((bf16[64,8,128]{2,0,1:T(8,128)(2,1)}), bf16[64,8,128]{2,0,1:T(8,128)(2,1)S(1)}, u32[]{:S(2)}, u32[]{:S(2)}) async-start(bf16[64,8,128]{2,0,1:T(8,128)(2,1)} %copy.45), calls=%async_computation.2 | async-start | bytes 262144 | tf_op jit(solution)/shard_map/all_to_all | solution.py:40
  22.6 28.1 %all-to-all-start = ((bf16[64,128,128]{2,0,1:T(8,128)(2,1)}), bf16[64,128,128]{2,0,1:T(8,128)(2,1)S(1)}, u32[]{:S(2)}, u32[]{:S(2)}) async-start(bf16[64,128,128]{2,0,1:T(8,128)(2,1)} %pad_maximum_fusion), calls=%async_computation | async-start | bytes 4194304 | tf_op jit(solution)/shard_map/all_to_all | solution.py:38
  58.2 5.7 %copy-start = (f32[2,64,16,2048]{3,2,1,0:T(8,128)}, f32[2,64,16,2048]{3,2,1,0:T(8,128)S(1)}, u32[]{:S(2)}) copy-start(f32[2,64,16,2048]{3,2,1,0:T(8,128)S(1)} %get-tuple-element.268) | copy-start | bytes 50331652 | tf_op jit(solution)/shard_map/while
  83.0 5.7 %copy-start = (f32[2,64,16,2048]{3,2,1,0:T(8,128)}, f32[2,64,16,2048]{3,2,1,0:T(8,128)S(1)}, u32[]{:S(2)}) copy-start(f32[2,64,16,2048]{3,2,1,0:T(8,128)S(1)} %get-tuple-element.268) | copy-start | bytes 50331652 | tf_op jit(solution)/shard_map/while
  107.9 5.7 %copy-start = (f32[2,64,16,2048]{3,2,1,0:T(8,128)}, f32[2,64,16,2048]{3,2,1,0:T(8,128)S(1)}, u32[]{:S(2)}) copy-start(f32[2,64,16,2048]{3,2,1,0:T(8,128)S(1)} %get-tuple-element.268) | copy-start | bytes 50331652 | tf_op jit(solution)/shard_map/while
  132.8 5.7 %copy-start = (f32[2,64,16,2048]{3,2,1,0:T(8,128)}, f32[2,64,16,2048]{3,2,1,0:T(8,128)S(1)}, u32[]{:S(2)}) copy-start(f32[2,64,16,2048]{3,2,1,0:T(8,128)S(1)} %get-tuple-element.268) | copy-start | bytes 50331652 | tf_op jit(solution)/shard_map/while
  151.9 24.1 %all-to-all-start.3 = ((f32[64,1,128]{2,1,0:T(1,128)}), f32[64,1,128]{2,1,0:T(1,128)S(1)}, u32[]{:S(2)}, u32[]{:S(2)}) async-start(f32[64,1,128]{2,1,0:T(1,128)} %reshape.162), calls=%async_computation.3 | async-start | bytes 65536 | tf_op jit(solution)/shard_map/all_to_all | solution.py:103
  191.8 99.2 %all-to-all-start.4 = ((f32[256,32,128]{2,1,0:T(8,128)}), f32[256,32,128]{2,1,0:T(8,128)}, u32[]{:S(2)}, u32[]{:S(2)}) async-start(f32[256,32,128]{2,1,0:T(8,128)} %bitcast.12), calls=%async_computation.4 | async-start | bytes 8388608 | tf_op jit(solution)/shard_map/all_to_all | solution.py:102
where the time goes:
time: 298 us; the launch traced here: 295 us
  waiting for transfers between devices  121 us (41%)
  matrix products  52.7 us (18%)
  other arithmetic  42.2 us (14%)
  starting transfers between devices  30.8 us (10%)
  local copies, waits for them, and re-layouts  30.8 us (10%)
  blocking collectives  15.8 us (5%)
    all_to_all x1, waiting for transfers between devices, body(): lax.all_to_all(outputs, 'context', split_axis=0, concat_axis=0, tiled=True)  91.2 us
    dot_general x4, matrix products, partial_value(): jnp.einsum('rkgc,ckd->rkgd', cache_weights, cache_values, preferred_eleme...  31.2 us
    all_to_all x1, waiting for transfers between devices, body(): lax.all_to_all(turned_q, 'tensor', split_axis=1, concat_axis=0, tiled=True)  19.2 us
    reduce_sum x4, other arithmetic, partial_value(): cache_weights.astype(jnp.float32).sum(-1)  17.3 us
    all_to_all x1, blocking collectives, body(): lax.all_to_all(totals, 'context', split_axis=0, concat_axis=0, tiled=True)  15.8 us
    all_to_all x1, starting transfers between devices, body(): lax.all_to_all(peaks, 'context', split_axis=0, concat_axis=0, tiled=True)  12.2 us
    dot_general x4, matrix products, partial_value(): jnp.einsum('rkgd,ckd->rkgc', grouped, cache_keys, preferred_element_type=...  11 us
    all_to_all x1, waiting for transfers between devices, body(): lax.all_to_all(peaks, 'context', split_axis=0, concat_axis=0, tiled=True)  10.8 us
  transfers between devices with their start and end apart: 5, of which 3 were waited for; matrix products, arithmetic and copies ran while one was open for 6% of the time, Pallas kernels for 0%

commit v1 on v0

v1 whole, which is shorter than its diff:
```python
import functools
import math

import jax
import jax.numpy as jnp
from jax import lax
from jax.experimental import pallas as pl
from jax.experimental.pallas import tpu as pltpu
from jax.sharding import PartitionSpec as P

SCALE = math.log2(math.e) / math.sqrt(128.0)
BF = jnp.bfloat16
F32 = jnp.float32
MIB = 2**20
KEY_BLOCK = 512
SUB = 256


def linear(z, x, y, core):
    y = y % 4
    return ((z % 8) * 8 + (x % 4) * 2 + y // 2) * 4 + (y % 2) * 2 + core % 2


def shift(dy, dcore):
    return [
        (linear(z, x, y, k), linear(z, x, y + dy, k + dcore))
        for z in range(8)
        for x in range(4)
        for y in range(4)
        for k in range(2)
    ]


def dot_nt(a, b):
    return lax.dot_general(a, b, (((1,), (1,)), ((), ())), preferred_element_type=F32)


def dot_nn(a, b):
    return jnp.dot(a, b, preferred_element_type=F32)


def turn_kernel(slots, cos_ref, sin_ref, *refs, with_kv):
    count = 16
    i = pl.program_id(0)
    ins, refs = refs[:4], refs[4:]
    kvs, outs = (refs[:4], refs[4:]) if with_kv else (None, refs)
    cosine = cos_ref[...][:, None, :]
    sine = sin_ref[...][:, None, :]
    start = pl.multiple_of(i * count * 16, count * 16)
    for j in range(4):
        wide = ins[j][...].astype(F32)
        flat = wide.reshape(count * 16, 128)
        turned = pltpu.roll(flat, 64, 1).reshape(count, 16, 128)
        value = (wide * cosine + turned * sine).astype(BF)
        outs[j][pl.ds(start, count * 16), :] = value.reshape(count * 16, 128)
    if with_kv:

        @pl.when(i == 0)
        def _():
            for j in range(4):
                outs[j][1024:1280, :] = kvs[j][...].reshape(256, 128)


def turn(queries, cosine, sine, kv, slots, head):
    with_kv = kv is not None
    rows = 1280 if with_kv else 1024

    def q_spec(j):
        return pl.BlockSpec((16, 16, 128), lambda i, s: (i, 2 * s[j] + head, 0))

    def kv_spec(j):
        return pl.BlockSpec((2, 2, 64, 128), lambda i, s: (s[j], 0, 0, 0))

    in_specs = [pl.BlockSpec((16, 128), lambda i, s: (i, 0))] * 2
    in_specs += [q_spec(j) for j in range(4)]
    args = [cosine, sine] + [queries] * 4
    if with_kv:
        in_specs += [kv_spec(j) for j in range(4)]
        args += [kv] * 4
    return pl.pallas_call(
        functools.partial(turn_kernel, with_kv=with_kv),
        grid_spec=pltpu.PrefetchScalarGridSpec(
            num_scalar_prefetch=1,
            grid=(4,),
            in_specs=in_specs,
            out_specs=[pl.BlockSpec((rows, 128), lambda i, s: (0, 0))] * 4,
        ),
        out_shape=[jax.ShapeDtypeStruct((rows, 128), BF)] * 4,
        compiler_params=pltpu.CompilerParams(vmem_limit_bytes=24 * MIB),
        name="turn%d" % head,
    )(slots, *args)


def eye_mask(rows):
    row = lax.broadcasted_iota(jnp.int32, (rows, 128), 0)
    lane = lax.broadcasted_iota(jnp.int32, (rows, 128), 1)
    return row, lane


def attend_kernel(slots, length, q0, q1, q2, q3, k_ref, v_ref, o_ref, q_s, k_s, v_s, st_s):
    j = pl.program_id(0)

    @pl.when(j == 0)
    def _():
        row = lax.broadcasted_iota(jnp.int32, (2048, 128), 0)
        live = row < length[0]
        first = k_ref[0:1, :].astype(F32)
        k_s[...] = jnp.where(live, k_ref[...].astype(F32), first).astype(BF)
        v_s[:, 0:128] = jnp.where(live, v_ref[...].astype(F32), 0.0).astype(BF)
        v_s[:, 128:256] = jnp.where(live, 1.0, 0.0).astype(BF)

    for n, ref in enumerate((q0, q1, q2, q3)):

        @pl.when(j == n)
        def _():
            q_s[...] = ref[...]

    slot = slots[j]
    row, lane = eye_mask(64)
    for s in range(4):
        q = q_s[s * SUB : (s + 1) * SUB, :]
        peak = None
        for b in range(2048 // KEY_BLOCK):
            keys = slice(b * KEY_BLOCK, (b + 1) * KEY_BLOCK)
            scores = dot_nt(q, k_s[keys, :])
            top = jnp.ceil(jnp.max(scores, axis=1, keepdims=True) * SCALE)
            new = top if peak is None else jnp.maximum(peak, top)
            weights = jnp.exp2(scores * SCALE - new).astype(BF)
            part = dot_nn(weights, v_s[keys, :])
            acc = part if peak is None else acc * jnp.exp2(peak - new) + part
            peak = new
        zrow = pl.multiple_of((2 * slot + s // 2) * 64, 64)
        for d in range(4):
            dest = 4 * (s % 2) + d
            rows = slice(d * 64, (d + 1) * 64)
            o_ref[dest, pl.ds(zrow, 64), :] = acc[rows, 0:128].astype(BF)
            pair = jnp.where(
                lane == row, peak[rows, :], jnp.where(lane == row + 64, acc[rows, 128:256], 0.0)
            )
            st_s[dest, pl.ds(2 * slot + s // 2, 1), :] = jnp.sum(pair, axis=0, keepdims=True)

    @pl.when(j == 3)
    def _():
        for dest in range(8):
            stats = st_s[dest]
            high = stats.astype(BF).astype(F32)
            o_ref[dest, 512:528, :] = jnp.concatenate([high, stats - high], axis=0).astype(BF)


def attend(qs, keys, values, slots, length, head):
    whole = lambda j, s, n: (0, 0)
    cache = pl.BlockSpec((None, 2048, 128), lambda j, s, n: (head, 0, 0))
    return pl.pallas_call(
        attend_kernel,
        grid_spec=pltpu.PrefetchScalarGridSpec(
            num_scalar_prefetch=2,
            grid=(4,),
            in_specs=[pl.BlockSpec((1024, 128), whole)] * 4 + [cache, cache],
            out_specs=pl.BlockSpec((8, 528, 128), lambda j, s, n: (0, 0, 0)),
            scratch_shapes=[
                pltpu.VMEM((1024, 128), BF),
                pltpu.VMEM((2048, 128), BF),
                pltpu.VMEM((2048, 256), BF),
                pltpu.VMEM((8, 8, 128), F32),
            ],
        ),
        out_shape=jax.ShapeDtypeStruct((8, 528, 128), BF),
        compiler_params=pltpu.CompilerParams(vmem_limit_bytes=40 * MIB),
        cost_estimate=pl.CostEstimate(
            flops=4 * 4096 * 2048 * 128, bytes_accessed=4 * MIB, transcendentals=4096 * 2048
        ),
        name="attend%d" % head,
    )(slots, length, *qs, keys, values)


def weigh(stats):
    peak = functools.reduce(jnp.maximum, stats)
    factors = [jnp.exp2(s - peak) for s in stats]
    sums = [pltpu.roll(s, 64, 1) for s in stats]
    return peak, factors, sums


def spread(pairs, row, lane):
    hit = (lane == row) | (lane == row + 64)
    return jnp.concatenate([jnp.where(hit, p, 0.0) for p in pairs], axis=1)


def pair_up(first, second, lane):
    return jnp.where(lane[0:1] < 64, first, pltpu.roll(second, 64, 1))


def fold_kernel(a_ref, b_ref, o_ref):
    row, lane = eye_mask(64)
    lane8 = lax.broadcasted_iota(jnp.int32, (8, 128), 1)
    tile = lax.broadcasted_iota(jnp.int32, (16, 128), 0)
    news = []
    for h, ref in enumerate((a_ref, b_ref)):
        stats = []
        for src in range(8):
            block = ref[src, 512:528, :].astype(F32)
            stats.append(block[0:8] + block[8:16])
        peak, factors, sums = weigh(stats)
        factors = [f.astype(BF).astype(F32) for f in factors]
        total = functools.reduce(jnp.add, [f * s for f, s in zip(factors, sums)])
        rolled = [pltpu.roll(f, 64, 1) for f in factors]
        joined = [jnp.where(lane8 < 64, factors[2 * p], rolled[2 * p + 1]) for p in range(4)]
        for z in range(8):
            mix = spread([x[z : z + 1] for x in joined], row, lane).astype(BF)
            parts = ref[:, z * 64 : z * 64 + 64, :].reshape(512, 128)
            o_ref[z, h * 64 : h * 64 + 64, :] = dot_nn(mix, parts).astype(BF)
        new = jnp.where(lane8 < 64, peak, pltpu.roll(total, 64, 1))
        high = new.astype(BF).astype(F32)
        news += [high, new - high]
    for z in range(8):
        value = jnp.zeros((16, 128), F32)
        for n, x in enumerate(news):
            value = jnp.where(tile == n, x[z : z + 1], value)
        o_ref[z, 128:144, :] = value.astype(BF)


def fold(first, second):
    return pl.pallas_call(
        fold_kernel,
        out_shape=jax.ShapeDtypeStruct((8, 144, 128), BF),
        compiler_params=pltpu.CompilerParams(vmem_limit_bytes=24 * MIB),
        name="fold",
    )(first, second)


def prompt_kernel(where, slots, *refs):
    q_refs, kv_refs, o_ref, st_ref = refs[:8], refs[8:12], refs[12], refs[13]
    row, lane = eye_mask(64)
    query = where[1] * 4 + lax.broadcasted_iota(jnp.int32, (64, 64), 0) // 16
    column = lax.broadcasted_iota(jnp.int32, (64, 64), 1)
    mine = where[1] // 16
    for h in range(2):
        q = q_refs[4 * h][...]
        for j in range(1, 4):
            q = jnp.where(slots[j] == mine, q_refs[4 * h + j][...], q)
        scores = []
        for j in range(4):
            part = dot_nt(q, kv_refs[j][h * 128 : h * 128 + 64, :]) * SCALE
            seen = column + slots[j] * 64 <= query
            scores.append(jnp.where(seen, part, -jnp.inf))
        top = functools.reduce(jnp.maximum, [jnp.max(s, axis=1, keepdims=True) for s in scores])
        top = jnp.ceil(top)
        acc = jnp.zeros((64, 128), F32)
        total = jnp.zeros((64, 1), F32)
        for j in range(4):
            weights = jnp.exp2(scores[j] - top).astype(BF)
            total = total + jnp.sum(weights.astype(F32), axis=1, keepdims=True)
            acc = acc + dot_nn(weights, kv_refs[j][h * 128 + 64 : h * 128 + 128, :])
        o_ref[h] = acc.astype(BF)
        pair = jnp.where(lane == row, top, jnp.where(lane == row + 64, total, 0.0))
        st_ref[h] = jnp.broadcast_to(jnp.sum(pair, axis=0, keepdims=True), (8, 128))


def prompt_part(q_first, q_second, where, slots):
    q_spec = pl.BlockSpec((64, 128), lambda i, w, s: (w[0], 0))
    kv_spec = pl.BlockSpec((256, 128), lambda i, w, s: (4, 0))
    return pl.pallas_call(
        prompt_kernel,
        grid_spec=pltpu.PrefetchScalarGridSpec(
            num_scalar_prefetch=2,
            grid=(1,),
            in_specs=[q_spec] * 8 + [kv_spec] * 4,
            out_specs=[
                pl.BlockSpec((2, 64, 128), lambda i, w, s: (0, 0, 0)),
                pl.BlockSpec((2, 8, 128), lambda i, w, s: (0, 0, 0)),
            ],
        ),
        out_shape=[
            jax.ShapeDtypeStruct((2, 64, 128), BF),
            jax.ShapeDtypeStruct((2, 8, 128), F32),
        ],
        compiler_params=pltpu.CompilerParams(vmem_limit_bytes=16 * MIB),
        name="prompt",
    )(where, slots, *q_first, *q_second, *q_second)


def final_kernel(got_ref, po_ref, pst_ref, o_ref):
    row, lane = eye_mask(64)
    for h in range(2):
        stats = []
        for src in range(8):
            block = got_ref[src, 128:144, :].astype(F32)
            stats.append(block[2 * h : 2 * h + 1] + block[2 * h + 1 : 2 * h + 2])
        stats.append(pst_ref[h][0:1])
        peak, factors, sums = weigh(stats)
        total = functools.reduce(jnp.add, [f * s for f, s in zip(factors, sums)])
        inverse = 1.0 / jnp.where(lane[0:1] < 64, total, 1.0)
        factors = [f * inverse for f in factors]
        factors.append(jnp.zeros_like(inverse))
        mix = spread([pair_up(factors[2 * p], factors[2 * p + 1], lane) for p in range(5)], row, lane)
        parts = got_ref[:, h * 64 : h * 64 + 64, :].reshape(512, 128)
        parts = jnp.concatenate([parts, po_ref[h], jnp.zeros((64, 128), BF)], axis=0)
        high = mix.astype(BF)
        low = (mix - high.astype(F32)).astype(BF)
        out = dot_nn(high, parts) + dot_nn(low, parts)
        o_ref[:, h * 16 : h * 16 + 16, :] = out.astype(BF).reshape(4, 16, 128)


def final(got, part_out, part_stats):
    return pl.pallas_call(
        final_kernel,
        out_shape=jax.ShapeDtypeStruct((4, 32, 128), BF),
        compiler_params=pltpu.CompilerParams(vmem_limit_bytes=16 * MIB),
        name="final",
    )(got, part_out, part_stats)


def body(
    queries,
    prompt_keys,
    prompt_values,
    cache_keys,
    cache_values,
    cache_lengths,
    offset,
    prompt_positions,
):
    axes = ("context", "tensor")
    context = lax.axis_index("context").astype(jnp.int32)
    tensor = lax.axis_index("tensor").astype(jnp.int32)
    core = tensor % 2
    other = 2 * (1 - tensor // 2)
    sends = jnp.stack([tensor, tensor ^ 1, other + core, other + 1 - core])
    slots = sends

    position = offset[0] + prompt_positions
    freq = jnp.exp(jnp.arange(64, dtype=F32) * (-2.0 * math.log(500000.0) / 128))
    angle = position.astype(F32)[:, None] * freq[None, :]
    cosine = jnp.cos(angle)
    sine = jnp.sin(angle)
    cosine = jnp.concatenate([cosine, cosine], axis=1)
    sine = jnp.concatenate([-sine, sine], axis=1)
    wide = prompt_keys.astype(F32)
    turned = wide * cosine[:, None, :] + jnp.roll(wide, 64, axis=-1) * sine[:, None, :]
    kv = jnp.stack([turned.astype(BF), prompt_values]).transpose(2, 0, 1, 3)

    def exchange(parts):
        own, swap, ahead, back = parts
        return (
            own,
            lax.ppermute(swap, axes, shift(0, 1)),
            lax.ppermute(ahead, axes, shift(1, 0)),
            lax.ppermute(back, axes, shift(-1, 1)),
        )

    q_first = exchange(turn(queries, cosine, sine, None, sends, 0))
    q_second = exchange(turn(queries, cosine, sine, kv, sends, 1))

    keys = cache_keys.transpose(1, 0, 2)
    values = cache_values.transpose(1, 0, 2)

    plane = [[z * 8 + r for r in range(8)] for z in range(8)]
    column = [[z * 8 + r for z in range(8)] for r in range(8)]

    def swap(parts, groups):
        return lax.all_to_all(
            parts, "context", split_axis=0, concat_axis=0, axis_index_groups=groups, tiled=True
        )

    first = swap(attend(q_first, keys, values, slots, cache_lengths, 0), plane)
    second = swap(attend(q_second, keys, values, slots, cache_lengths, 1), plane)
    where = jnp.stack([context % 16, context])
    part_out, part_stats = prompt_part(q_first, q_second, where, slots)
    got = swap(fold(first, second), column)
    return final(got, part_out, part_stats)


def solution(mesh):
    in_specs = (
        P("tensor", None, None),
        P("tensor", None, None),
        P("tensor", None, None),
        P("context", "tensor", None),
        P("context", "tensor", None),
        P("context"),
        P(),
        P("tensor"),
    )
    out_specs = P("context", "tensor", None)
    return jax.shard_map(body, mesh=mesh, in_specs=in_specs, out_specs=out_specs, check_vma=False)
```

time: 298 us -> 117 us (0.39)
  waiting for transfers between devices: 121 us -> 30.7 us
  matrix products: 52.7 us -> 0 us
  other arithmetic: 42.2 us -> 2.35 us
  Pallas kernels: 0 us -> 31.4 us
  local copies, waits for them, and re-layouts: 30.8 us -> 8.82 us
  starting transfers between devices: 30.8 us -> 19.7 us
  blocking collectives: 15.8 us -> 21.9 us
    all_to_all x5 -> x2, waiting for transfers between devices: 121 us -> 9.23 us  [swap(): lax.all_to_all(parts, 'context', split_axis=0, concat_axis=0, axis_index_...]
    dot_general x16 -> x0, matrix products: 52.7 us -> none  [the longest x4 31.2 us: partial_value(): jnp.einsum('rkgc,ckd->rkgd', cache_weights, cache_values, preferred_eleme...]
    pallas_call x0 -> x7, Pallas kernels: none -> 31.4 us  [the longest x2 24.9 us: attend(): pl.pallas_call(attend_kernel, grid_spec=pltpu.PrefetchScalarGridSpec(num_...]
    ppermute x0 -> x6, waiting for transfers between devices: none -> 21.4 us  [the longest x2 18.4 us: exchange(): lax.ppermute(ahead, axes, shift(1, 0))]
    reduce_sum x10 -> x0, other arithmetic: 21.4 us -> none  [the longest x4 17.3 us: partial_value(): cache_weights.astype(jnp.float32).sum(-1)]
    all_to_all x5 -> x2, starting transfers between devices: 30.8 us -> 14.5 us  [swap(): lax.all_to_all(parts, 'context', split_axis=0, concat_axis=0, axis_index_...]
    dynamic_update_slice x8 -> x0, local copies, waits for them, and re-layouts: 9.65 us -> none  [body(): outputs, peaks, totals = lax.map(one_block, (blocked, starts))]
    all_to_all x1, blocking collectives: 15.8 us -> 21.9 us  [swap(): lax.all_to_all(parts, 'context', split_axis=0, concat_axis=0, axis_index_...]
  transfers between devices with their start and end apart: 5 -> 8, of which waited for: 3 -> 5; matrix products, arithmetic and copies ran while one was open for 6% -> 3% of each run, Pallas kernels for 0% -> 13%
where the time goes in v1:
time: 117 us; the launch traced here: 116 us
  Pallas kernels  31.4 us (27%)
  waiting for transfers between devices  30.7 us (26%)
  blocking collectives  21.9 us (19%)
  starting transfers between devices  19.7 us (17%)
  local copies, waits for them, and re-layouts  8.82 us (8%)
  other arithmetic  2.35 us (2%)
  between operations  1.55 us (1%)
    pallas_call x2, Pallas kernels, attend(): pl.pallas_call(attend_kernel, grid_spec=pltpu.PrefetchScalarGridSpec(num_...  24.9 us
    all_to_all x1, blocking collectives, swap(): lax.all_to_all(parts, 'context', split_axis=0, concat_axis=0, axis_index_...  21.9 us
    ppermute x2, waiting for transfers between devices, exchange(): lax.ppermute(ahead, axes, shift(1, 0))  18.4 us
    all_to_all x2, starting transfers between devices, swap(): lax.all_to_all(parts, 'context', split_axis=0, concat_axis=0, axis_index_...  14.5 us
    all_to_all x2, waiting for transfers between devices, swap(): lax.all_to_all(parts, 'context', split_axis=0, concat_axis=0, axis_index_...  9.23 us
    unnamed x41, local copies, waits for them, and re-layouts  7.65 us
    ppermute x2, starting transfers between devices, exchange(): lax.ppermute(ahead, axes, shift(1, 0))  4.34 us
    ppermute x2, waiting for transfers between devices, exchange(): lax.ppermute(back, axes, shift(-1, 1))  3.06 us
  transfers between devices with their start and end apart: 8, of which 5 were waited for; matrix products, arithmetic and copies ran while one was open for 3% of the time, Pallas kernels for 13%

profile of v1, /device:TPU:8, one launch (start us, length us, event | category | flops | bytes accessed | tf_op | source)
XLA Modules:
  0.0 116.3 jit_solution(13866464320273280633)
XLA Ops:
  0.7 0.7 add_convert_fusion
  1.3 0.2 fusion.3
  1.5 0.1 pad_maximum_fusion
  1.6 0.0 copy-start.7
  1.7 0.1 pad_add_fusion.slots
  1.7 0.0 copy-start
  1.7 1.6 %copy-done = bf16[64,128,128]{2,1,0:T(8,128)(2,1)S(1)} copy-done((bf16[64,128,128]{2,1,0:T(8,128)(2,1)S(1)}, bf16[64,128,128]{2,1,0:T(8,128)(2,1)}, u32[]{:S(2)}) %copy-start) | copy-done | bytes 2097176
  3.3 0.0 copy-start.17
  3.3 0.0 copy-start.18
  3.3 1.5 %turn0.1 = (bf16[1024,128]{1,0:T(8,128)(2,1)S(1)}, bf16[1024,128]{1,0:T(8,128)(2,1)S(1)}, bf16[1024,128]{1,0:T(8,128)(2,1)S(1)}, bf16[1024,128]{1,0:T(8,128)(2,1)S(1)}) custom-call(s32[4]{0:T(128)S(1)} %pad_add_fusion.slots, f32[64,128]{1,0:T(8,128)S(1)} %get-tuple-element.30.cos_ref, f32[64,128]{1,0:T(8,128)S(1)} %get-tuple-element.31.sin_ref, ...), custom_call_target="tpu_custom_call" | custom-call | tf_op jit(solution)/shard_map/turn0/pallas_call | solution.py:80
  4.8 0.0 copy-start.9
  4.8 0.1 collective-permute-start
  4.9 1.7 %collective-permute-start.1 = (bf16[1024,128]{1,0:T(8,128)(2,1)S(1)}, bf16[1024,128]{1,0:T(8,128)(2,1)S(1)}, u32[]{:S(2)}, u32[]{:S(2)}) collective-permute-start(bf16[1024,128]{1,0:T(8,128)(2,1)S(1)} %get-tuple-element.17), channel_id=1, source_target_pairs={{0,2},{1,3},{2,4},{3,5},{4,6},{5,7},{6,0},{7,1},{8,10},{9,11},{10,... | collective-permute-start | bytes 786440 | tf_op jit(solution)/shard_map/ppermute | solution.py:346
  6.6 0.0 copy-start.19
  6.6 0.6 collective-permute-start.2
  7.2 0.0 copy-done.17
  7.2 0.0 copy-done.18
  7.2 0.3 copy_bitcast_fusion
  7.5 0.0 copy-done.19
  7.5 0.0 copy-start.3
  8.2 0.9 fusion.4
  9.1 0.0 collective-permute-done.q1.refs_1_
  9.1 0.0 copy-start.11
  9.1 4.9 %collective-permute-done.1.q2.refs_2_ = bf16[1024,128]{1,0:T(8,128)(2,1)S(1)} collective-permute-done((bf16[1024,128]{1,0:T(8,128)(2,1)S(1)}, bf16[1024,128]{1,0:T(8,128)(2,1)S(1)}, u32[]{:S(2)}, u32[]{:S(2)}) %collective-permute-start.1) | collective-permute-done | bytes 262176 | tf_op jit(solution)/shard_map/ppermute | solution.py:346
  14.1 0.8 collective-permute-done.2.q3.refs_3_
  14.9 0.0 copy-done.9
  14.9 0.0 copy-done.3
  14.9 12.5 %attend0.1 = bf16[8,528,128]{2,1,0:T(8,128)(2,1)S(1)} custom-call(s32[4]{0:T(128)S(1)} %pad_add_fusion.slots, s32[1]{0:T(128)S(6)} %copy.20.length, bf16[1024,128]{1,0:T(8,128)(2,1)S(1)} %get-tuple-element.15.q0.refs_0_, bf16[1024,128]{1,0:T(8,128)(2,1)S(1)} %collective-permute-done.q1.refs_1_, bf16[1024,128]{1,0:T(8,128)(2,1)S(1)} %collective-permute-done.1.q2.refs_2_, ...), custom_call_target="tpu_custom_call" | custom-call | flops 4294967296 | bytes 4194304 | tf_op jit(solution)/shard_map/attend0/pallas_call | solution.py:153
  27.3 0.0 copy-done.11
  27.4 0.0 copy-start.2
  27.4 1.0 copy-done.2
  28.3 0.0 copy-start.5
  28.3 1.0 copy-done.5
  29.3 0.7 copy-done.13
  30.0 0.7 copy-done.15
  30.7 6.1 %all-to-all-start = ((bf16[8,528,128]{2,1,0:T(8,128)(2,1)}), bf16[8,528,128]{2,1,0:T(8,128)(2,1)S(1)}, u32[]{:S(2)}, u32[]{:S(2)}) async-start(bf16[8,528,128]{2,1,0:T(8,128)(2,1)} %copy-done.2), calls=%async_computation | async-start | bytes 2162688 | tf_op jit(solution)/shard_map/all_to_all | solution.py:360
  36.8 0.0 copy-done.7
  36.8 1.2 %fusion.2 = bf16[1,64,8,128]{3,1,0,2:T(8,128)(2,1)S(1)} fusion(f32[64,8,64]{2,0,1:T(8,128)} %get-tuple-element.26, f32[64,8,64]{2,0,1:T(8,128)} %get-tuple-element.25, f32[64,128]{1,0:T(8,128)S(1)} %get-tuple-element.31.sin_ref, f32[64,128]{1,0:T(8,128)S(1)} %get-tuple-element.30.cos_ref, bf16[64,8,128]{2,1,0:T(8,128)(2,1)} %param.9), kind=kLoop, calls=%fused_computation.6 | loop fusion | flops 393216 | bytes 589824 | tf_op jit(solution)/shard_map/stack | solution.py:339
  38.0 0.9 copy.19
  39.0 0.0 copy-done.1
  39.0 0.0 copy-start.8
  39.0 0.7 copy-done.8
  39.8 1.5 %turn1.1 = (bf16[1280,128]{1,0:T(8,128)(2,1)S(1)}, bf16[1280,128]{1,0:T(8,128)(2,1)S(1)}, bf16[1280,128]{1,0:T(8,128)(2,1)S(1)}, bf16[1280,128]{1,0:T(8,128)(2,1)S(1)}) custom-call(s32[4]{0:T(128)S(1)} %pad_add_fusion.slots, f32[64,128]{1,0:T(8,128)S(1)} %get-tuple-element.30.cos_ref, f32[64,128]{1,0:T(8,128)S(1)} %copy-done.8, ...), custom_call_target="tpu_custom_call" | custom-call | tf_op jit(solution)/shard_map/turn1/pallas_call | solution.py:80
  41.3 0.1 collective-permute-start.3
  41.4 2.7 %collective-permute-start.4 = (bf16[1280,128]{1,0:T(8,128)(2,1)S(1)}, bf16[1280,128]{1,0:T(8,128)(2,1)S(1)}, u32[]{:S(2)}, u32[]{:S(2)}) collective-permute-start(bf16[1280,128]{1,0:T(8,128)(2,1)S(1)} %get-tuple-element.21), channel_id=1, source_target_pairs={{0,2},{1,3},{2,4},{3,5},{4,6},{5,7},{6,0},{7,1},{8,10},{9,11},{10,... | collective-permute-start | bytes 983048 | tf_op jit(solution)/shard_map/ppermute | solution.py:346
  44.1 0.0 collective-permute-start.5
  44.1 0.0 collective-permute-done.3.q1.refs_5_.refs_9_
  44.1 13.4 %collective-permute-done.4.q2.refs_6_.refs_10_ = bf16[1280,128]{1,0:T(8,128)(2,1)S(1)} collective-permute-done((bf16[1280,128]{1,0:T(8,128)(2,1)S(1)}, bf16[1280,128]{1,0:T(8,128)(2,1)S(1)}, u32[]{:S(2)}, u32[]{:S(2)}) %collective-permute-start.4) | collective-permute-done | bytes 327712 | tf_op jit(solution)/shard_map/ppermute | solution.py:346
  57.5 2.3 %collective-permute-done.5.q3.refs_7_.refs_11_ = bf16[1280,128]{1,0:T(8,128)(2,1)S(1)} collective-permute-done((bf16[1280,128]{1,0:T(8,128)(2,1)S(1)}, bf16[1280,128]{1,0:T(8,128)(2,1)S(1)}, u32[]{:S(2)}, u32[]{:S(2)}) %collective-permute-start.5) | collective-permute-done | bytes 327712 | tf_op jit(solution)/shard_map/ppermute | solution.py:347
  59.8 0.0 copy-done.4
  59.8 0.0 copy-done.6
  59.8 12.4 %attend1.1 = bf16[8,528,128]{2,1,0:T(8,128)(2,1)S(1)} custom-call(s32[4]{0:T(128)S(1)} %pad_add_fusion.slots, s32[1]{0:T(128)S(6)} %copy.20.length, bf16[1280,128]{1,0:T(8,128)(2,1)S(1)} %get-tuple-element.19.q0.refs_4_.refs_8_, bf16[1280,128]{1,0:T(8,128)(2,1)S(1)} %collective-permute-done.3.q1.refs_5_.refs_9_, ...), custom_call_target="tpu_custom_call" | custom-call | flops 4294967296 | bytes 4194304 | tf_op jit(solution)/shard_map/attend1/pallas_call | solution.py:153
  72.2 0.0 all-to-all-done.a_ref
  72.2 21.9 %all_to_all.15.b_ref = bf16[8,528,128]{2,1,0:T(8,128)(2,1)S(1)} all-to-all(bf16[8,528,128]{2,1,0:T(8,128)(2,1)S(1)} %attend1.1), channel_id=1, replica_groups={{0,4,8,12,16,20,24,28},{32,36,40,44,48,52,56,60},{64,68,72,76,80,84,88,..., dimensions={0} | all-to-all | bytes 2162688 | tf_op jit(solution)/shard_map/all_to_all | solution.py:360
  94.1 1.2 %fold.1 = bf16[8,144,128]{2,1,0:T(8,128)(2,1)} custom-call(bf16[8,528,128]{2,1,0:T(8,128)(2,1)S(1)} %all-to-all-done.a_ref, bf16[8,528,128]{2,1,0:T(8,128)(2,1)S(1)} %all_to_all.15.b_ref), custom_call_target="tpu_custom_call" | custom-call | tf_op jit(solution)/shard_map/fold/pallas_call | solution.py:222
  95.4 8.5 %all-to-all-start.2 = ((bf16[8,144,128]{2,1,0:T(8,128)(2,1)}), bf16[8,144,128]{2,1,0:T(8,128)(2,1)S(1)}, u32[]{:S(2)}, u32[]{:S(2)}) async-start(bf16[8,144,128]{2,1,0:T(8,128)(2,1)} %fold.1), calls=%async_computation.2 | async-start | bytes 589824 | tf_op jit(solution)/shard_map/all_to_all | solution.py:360
  103.9 0.1 pad_add_fusion.1.where
  103.9 0.0 copy-done.10
  103.9 0.0 copy-done.12
  103.9 0.0 copy-done.14
  103.9 0.9 copy-done.16
  104.9 1.2 %prompt.1 = (bf16[2,64,128]{2,1,0:T(8,128)(2,1)S(1)}, f32[2,8,128]{2,1,0:T(8,128)S(1)}) custom-call(s32[2]{0:T(128)S(1)} %pad_add_fusion.1.where, s32[4]{0:T(128)S(1)} %pad_add_fusion.slots, bf16[1024,128]{1,0:T(8,128)(2,1)S(1)} %copy-done.10, bf16[1024,128]{1,0:T(8,128)(2,1)S(1)} %copy-done.12, bf16[1024,128]{1,0:T(8,128)(2,1)S(1)} %copy-done.14, ...), custom_call_target="tpu_custom_call" | custom-call | tf_op jit(solution)/shard_map/prompt/pallas_call | solution.py:261
  106.1 9.2 %all-to-all-done.2.got_ref = bf16[8,144,128]{2,1,0:T(8,128)(2,1)S(1)} async-done(((bf16[8,144,128]{2,1,0:T(8,128)(2,1)}), bf16[8,144,128]{2,1,0:T(8,128)(2,1)S(1)}, u32[]{:S(2)}, u32[]{:S(2)}) %all-to-all-start.2) | async-done | bytes 294944 | tf_op jit(solution)/shard_map/all_to_all | solution.py:360
  115.3 1.0 final.1
  (12 shorter events, 0.1 us)
Async XLA Ops:
  1.6 35.2 %copy-start.7 = (f32[64,128]{1,0:T(8,128)}, f32[64,128]{1,0:T(8,128)S(1)}, u32[]{:S(2)}) copy-start(f32[64,128]{1,0:T(8,128)S(1)} %get-tuple-element.31.sin_ref) | copy-start | bytes 98308
  1.7 1.6 %copy-start = (bf16[64,128,128]{2,1,0:T(8,128)(2,1)S(1)}, bf16[64,128,128]{2,1,0:T(8,128)(2,1)}, u32[]{:S(2)}) copy-start(bf16[64,128,128]{2,1,0:T(8,128)(2,1)} %refs_3_.3) | copy-start | bytes 6291460
  3.3 3.9 %copy-start.17 = (bf16[2048,2,128]{2,1,0:T(2,128)(2,1)S(1)}, bf16[2048,2,128]{2,1,0:T(2,128)(2,1)}, u32[]{:S(2)}) copy-start(bf16[2048,2,128]{2,1,0:T(2,128)(2,1)} %param.12) | copy-start | bytes 3145732
  3.3 3.9 %copy-start.18 = (bf16[2048,2,128]{2,1,0:T(2,128)(2,1)S(1)}, bf16[2048,2,128]{2,1,0:T(2,128)(2,1)}, u32[]{:S(2)}) copy-start(bf16[2048,2,128]{2,1,0:T(2,128)(2,1)} %param.11) | copy-start | bytes 3145732
  4.8 10.0 %copy-start.9 = (bf16[1024,128]{1,0:T(8,128)(2,1)}, bf16[1024,128]{1,0:T(8,128)(2,1)S(1)}, u32[]{:S(2)}) copy-start(bf16[1024,128]{1,0:T(8,128)(2,1)S(1)} %get-tuple-element.15.q0.refs_0_) | copy-start | bytes 786436
  4.8 4.3 %collective-permute-start = (bf16[1024,128]{1,0:T(8,128)(2,1)S(1)}, bf16[1024,128]{1,0:T(8,128)(2,1)S(1)}, u32[]{:S(2)}, u32[]{:S(2)}) collective-permute-start(bf16[1024,128]{1,0:T(8,128)(2,1)S(1)} %get-tuple-element.16), channel_id=1, source_target_pairs={{0,1},{1,0},{2,3},{3,2},{4,5},{5,4},{6,7},{7,6},{8,9},{9,8},{10,11... | collective-permute-start | bytes 786440 | tf_op jit(solution)/shard_map/ppermute | solution.py:345
  4.9 9.1 %collective-permute-start.1 = (bf16[1024,128]{1,0:T(8,128)(2,1)S(1)}, bf16[1024,128]{1,0:T(8,128)(2,1)S(1)}, u32[]{:S(2)}, u32[]{:S(2)}) collective-permute-start(bf16[1024,128]{1,0:T(8,128)(2,1)S(1)} %get-tuple-element.17), channel_id=1, source_target_pairs={{0,2},{1,3},{2,4},{3,5},{4,6},{5,7},{6,0},{7,1},{8,10},{9,11},{10,... | collective-permute-start | bytes 786440 | tf_op jit(solution)/shard_map/ppermute | solution.py:346
  6.6 0.9 copy-start.19
  6.6 8.3 %collective-permute-start.2 = (bf16[1024,128]{1,0:T(8,128)(2,1)S(1)}, bf16[1024,128]{1,0:T(8,128)(2,1)S(1)}, u32[]{:S(2)}, u32[]{:S(2)}) collective-permute-start(bf16[1024,128]{1,0:T(8,128)(2,1)S(1)} %get-tuple-element.18), channel_id=1, source_target_pairs={{0,7},{1,6},{2,1},{3,0},{4,3},{5,2},{6,5},{7,4},{8,15},{9,14},{10,... | collective-permute-start | bytes 786440 | tf_op jit(solution)/shard_map/ppermute | solution.py:347
  7.5 7.4 %copy-start.3 = (bf16[2,2048,128]{2,1,0:T(8,128)(2,1)}, bf16[2,2048,128]{2,1,0:T(8,128)(2,1)S(1)}, u32[]{:S(2)}) copy-start(bf16[2,2048,128]{2,1,0:T(8,128)(2,1)S(1)} %get-tuple-element.32.v_ref) | copy-start | bytes 3145732
  9.1 18.2 %copy-start.11 = (bf16[1024,128]{1,0:T(8,128)(2,1)}, bf16[1024,128]{1,0:T(8,128)(2,1)S(1)}, u32[]{:S(2)}) copy-start(bf16[1024,128]{1,0:T(8,128)(2,1)S(1)} %collective-permute-done.q1.refs_1_) | copy-start | bytes 786436
  27.4 1.0 copy-start.2
  28.3 1.0 copy-start.5
  29.3 0.7 copy-start.13
  30.0 0.7 copy-start.15
  30.7 8.2 %copy-start.1 = (bf16[64,128,128]{2,1,0:T(8,128)(2,1)S(1)}, bf16[64,128,128]{2,1,0:T(8,128)(2,1)}, u32[]{:S(2)}) copy-start(bf16[64,128,128]{2,1,0:T(8,128)(2,1)} %refs_3_.3) | copy-start | bytes 6291460
  30.7 41.5 %all-to-all-start = ((bf16[8,528,128]{2,1,0:T(8,128)(2,1)}), bf16[8,528,128]{2,1,0:T(8,128)(2,1)S(1)}, u32[]{:S(2)}, u32[]{:S(2)}) async-start(bf16[8,528,128]{2,1,0:T(8,128)(2,1)} %copy-done.2), calls=%async_computation | async-start | bytes 2162688 | tf_op jit(solution)/shard_map/all_to_all | solution.py:360
  39.0 0.8 copy-start.8
  39.8 20.0 %copy-start.4 = (bf16[2,2048,128]{2,1,0:T(8,128)(2,1)S(1)}, bf16[2,2048,128]{2,1,0:T(8,128)(2,1)}, u32[]{:S(2)}) copy-start(bf16[2,2048,128]{2,1,0:T(8,128)(2,1)} %copy-done.3) | copy-start | bytes 3145732
  39.8 20.0 %copy-start.6 = (bf16[2,2048,128]{2,1,0:T(8,128)(2,1)S(1)}, bf16[2,2048,128]{2,1,0:T(8,128)(2,1)}, u32[]{:S(2)}) copy-start(bf16[2,2048,128]{2,1,0:T(8,128)(2,1)} %copy-done.5) | copy-start | bytes 3145732
  41.3 2.8 %collective-permute-start.3 = (bf16[1280,128]{1,0:T(8,128)(2,1)S(1)}, bf16[1280,128]{1,0:T(8,128)(2,1)S(1)}, u32[]{:S(2)}, u32[]{:S(2)}) collective-permute-start(bf16[1280,128]{1,0:T(8,128)(2,1)S(1)} %get-tuple-element.20), channel_id=1, source_target_pairs={{0,1},{1,0},{2,3},{3,2},{4,5},{5,4},{6,7},{7,6},{8,9},{9,8},{10,11... | collective-permute-start | bytes 983048 | tf_op jit(solution)/shard_map/ppermute | solution.py:345
  41.4 16.1 %collective-permute-start.4 = (bf16[1280,128]{1,0:T(8,128)(2,1)S(1)}, bf16[1280,128]{1,0:T(8,128)(2,1)S(1)}, u32[]{:S(2)}, u32[]{:S(2)}) collective-permute-start(bf16[1280,128]{1,0:T(8,128)(2,1)S(1)} %get-tuple-element.21), channel_id=1, source_target_pairs={{0,2},{1,3},{2,4},{3,5},{4,6},{5,7},{6,0},{7,1},{8,10},{9,11},{10,... | collective-permute-start | bytes 983048 | tf_op jit(solution)/shard_map/ppermute | solution.py:346
  44.1 15.7 %collective-permute-start.5 = (bf16[1280,128]{1,0:T(8,128)(2,1)S(1)}, bf16[1280,128]{1,0:T(8,128)(2,1)S(1)}, u32[]{:S(2)}, u32[]{:S(2)}) collective-permute-start(bf16[1280,128]{1,0:T(8,128)(2,1)S(1)} %get-tuple-element.22), channel_id=1, source_target_pairs={{0,7},{1,6},{2,1},{3,0},{4,3},{5,2},{6,5},{7,4},{8,15},{9,14},{10,... | collective-permute-start | bytes 983048 | tf_op jit(solution)/shard_map/ppermute | solution.py:347
  94.1 9.8 %copy-start.10 = (bf16[1024,128]{1,0:T(8,128)(2,1)S(1)}, bf16[1024,128]{1,0:T(8,128)(2,1)}, u32[]{:S(2)}) copy-start(bf16[1024,128]{1,0:T(8,128)(2,1)} %copy-done.9) | copy-start | bytes 786436
  94.1 9.8 %copy-start.12 = (bf16[1024,128]{1,0:T(8,128)(2,1)S(1)}, bf16[1024,128]{1,0:T(8,128)(2,1)}, u32[]{:S(2)}) copy-start(bf16[1024,128]{1,0:T(8,128)(2,1)} %copy-done.11) | copy-start | bytes 786436
  94.1 9.8 %copy-start.14 = (bf16[1024,128]{1,0:T(8,128)(2,1)S(1)}, bf16[1024,128]{1,0:T(8,128)(2,1)}, u32[]{:S(2)}) copy-start(bf16[1024,128]{1,0:T(8,128)(2,1)} %copy-done.13) | copy-start | bytes 786436
  95.4 19.9 %all-to-all-start.2 = ((bf16[8,144,128]{2,1,0:T(8,128)(2,1)}), bf16[8,144,128]{2,1,0:T(8,128)(2,1)S(1)}, u32[]{:S(2)}, u32[]{:S(2)}) async-start(bf16[8,144,128]{2,1,0:T(8,128)(2,1)} %fold.1), calls=%async_computation.2 | async-start | bytes 589824 | tf_op jit(solution)/shard_map/all_to_all | solution.py:360
  103.9 1.0 copy-start.16

commit v2 on v1

v2 whole, which is shorter than its diff:
```python
import functools
import math

import jax
import jax.numpy as jnp
import numpy as np
from jax import lax
from jax.experimental import pallas as pl
from jax.experimental.pallas import tpu as pltpu
from jax.sharding import PartitionSpec as P

SCALE = math.log2(math.e) / math.sqrt(128.0)
BF = jnp.bfloat16
F32 = jnp.float32
MIB = 2**20
BIG = 60 * MIB
KEY_BLOCK = 512
SUB = 256


def linear(z, x, y, core):
    y = y % 4
    return ((z % 8) * 8 + (x % 4) * 2 + y // 2) * 4 + (y % 2) * 2 + core % 2


def shift(dy, dcore):
    return [
        (linear(z, x, y, k), linear(z, x, y + dy, k + dcore))
        for z in range(8)
        for x in range(4)
        for y in range(4)
        for k in range(2)
    ]


def dot_nt(a, b):
    return lax.dot_general(a, b, (((1,), (1,)), ((), ())), preferred_element_type=F32)


def dot_nn(a, b):
    return jnp.dot(a, b, preferred_element_type=F32)


def slots_of():
    tensor = lax.axis_index("tensor").astype(jnp.int32)
    core = lax.rem(tensor, 2)
    other = 2 * (1 - lax.div(tensor, 2))
    return tensor, tensor + 1 - 2 * core, other + core, other + 1 - core


def turn_kernel(offset, pos_ref, freq_ref, k_ref, v_ref, q_ref, *refs):
    outs, (q_s, out_s, cos_s, sin_s, wide_s, in_sem, out_sem) = refs[:4], refs[4:]
    slots = slots_of()

    def fetch(j):
        heads = pl.ds(pl.multiple_of(slots[j] * 32, 32), 32)
        return pltpu.make_async_copy(q_ref.at[:, heads, :], q_s.at[j], in_sem.at[j])

    def send(j):
        return pltpu.make_async_copy(out_s.at[j], outs[j], out_sem.at[j])

    order = (2, 3, 1, 0)
    for j in order:
        fetch(j).start()
    row = lax.broadcasted_iota(jnp.int32, (64, 64), 0)
    column = lax.broadcasted_iota(jnp.int32, (64, 64), 1)
    position = (pos_ref[...] + offset[0]).astype(F32)
    position = jnp.sum(jnp.where(row == column, position, 0.0), axis=1, keepdims=True)
    angle = position * freq_ref[...]
    lane = lax.broadcasted_iota(jnp.int32, (64, 128), 1)
    cosine = jnp.cos(angle)
    sine = jnp.sin(angle)
    sine = jnp.where(lane < 64, -sine, sine)
    cos_s[...] = cosine
    sin_s[...] = sine
    wide = k_ref[...].astype(F32)
    rolled = pltpu.roll(wide.reshape(512, 128), 64, 1).reshape(64, 8, 128)
    wide_s[0] = (wide * cosine[:, None, :] + rolled * sine[:, None, :]).reshape(512, 128)
    wide_s[1] = v_ref[...].astype(F32).reshape(512, 128)
    for j in order:
        fetch(j).wait()

        @pl.loop(0, 4)
        def _(i):
            rows = pl.ds(pl.multiple_of(i * 16, 16), 16)
            cosine = cos_s[rows, :][:, None, :]
            sine = sin_s[rows, :][:, None, :]
            for head in range(2):
                wide = q_s[j, rows, head * 16 : head * 16 + 16, :].astype(F32)
                rolled = pltpu.roll(wide.reshape(256, 128), 64, 1).reshape(16, 16, 128)
                value = (wide * cosine + rolled * sine).reshape(256, 128).astype(BF)
                out_s[j, pl.ds(pl.multiple_of(head * 1024 + i * 256, 256), 256), :] = value

        for head in range(2):
            for n in range(2):
                start = 2048 + head * 128 + n * 64
                picked = wide_s[n, pl.ds(2 * slots[j] + head, 64, 8), :]
                out_s[j, start : start + 64, :] = picked.astype(BF)
        send(j).start()
    for j in order:
        send(j).wait()


def turn(queries, offset, positions, keys, values):
    freq = np.exp(np.arange(64, dtype=np.float32) * np.float32(-2.0 * math.log(500000.0) / 128))
    freq = jnp.asarray(np.concatenate([freq, freq])[None, :], F32)
    vmem = pl.BlockSpec(memory_space=pltpu.VMEM)
    hbm = pl.BlockSpec(memory_space=pl.ANY)
    return pl.pallas_call(
        turn_kernel,
        in_specs=[pl.BlockSpec(memory_space=pltpu.SMEM)] + [vmem] * 4 + [hbm],
        out_specs=[hbm] * 4,
        out_shape=[jax.ShapeDtypeStruct((2304, 128), BF)] * 4,
        scratch_shapes=[
            pltpu.VMEM((4, 64, 32, 128), BF),
            pltpu.VMEM((4, 2304, 128), BF),
            pltpu.VMEM((64, 128), F32),
            pltpu.VMEM((64, 128), F32),
            pltpu.VMEM((2, 512, 128), F32),
            pltpu.SemaphoreType.DMA((4,)),
            pltpu.SemaphoreType.DMA((4,)),
        ],
        compiler_params=pltpu.CompilerParams(vmem_limit_bytes=BIG),
        name="turn",
    )(offset, positions.reshape(1, 64), freq, keys, values, queries)


def lay_kernel(length, k_ref, v_ref, ko_ref, vo_ref, in_s, wide_s, out_s, in_sem, out_sem):
    refs, outs = (k_ref, v_ref), (ko_ref, vo_ref)

    def fetch(n, c):
        rows = pl.ds(c * 1024, 1024)
        return pltpu.make_async_copy(refs[n].at[rows, :], in_s.at[n, rows, :], in_sem.at[n, c])

    def send(n, c):
        rows = pl.ds(c * 512, 512)
        return pltpu.make_async_copy(
            out_s.at[n, :, rows, :], outs[n].at[:, rows, :], out_sem.at[n, c]
        )

    parts = [(n, c) for c in range(4) for n in range(2)]
    for n, c in parts:
        fetch(n, c).start()
    for n, c in parts:
        fetch(n, c).wait()
        live = lax.broadcasted_iota(jnp.int32, (512, 128), 0) + c * 512 < length[0]
        wide_s[n] = in_s[n, c * 1024 : c * 1024 + 1024, :].astype(F32)
        first = in_s[n, 0:16, :].astype(F32)
        for head in range(2):
            value = wide_s[n, pl.ds(head, 512, 2), :]
            dead = first[head : head + 1, :] if n == 0 else 0.0
            out_s[n, head, c * 512 : c * 512 + 512, :] = jnp.where(live, value, dead).astype(BF)
        send(n, c).start()
    for n, c in parts:
        send(n, c).wait()


def lay(keys, values, length):
    return pl.pallas_call(
        lay_kernel,
        in_specs=[pl.BlockSpec(memory_space=pltpu.SMEM)] + [pl.BlockSpec(memory_space=pl.ANY)] * 2,
        out_specs=[pl.BlockSpec(memory_space=pl.ANY)] * 2,
        out_shape=[jax.ShapeDtypeStruct((2, 2048, 128), BF)] * 2,
        scratch_shapes=[
            pltpu.VMEM((2, 4096, 128), BF),
            pltpu.VMEM((2, 1024, 128), F32),
            pltpu.VMEM((2, 2, 2048, 128), BF),
            pltpu.SemaphoreType.DMA((2, 4)),
            pltpu.SemaphoreType.DMA((2, 4)),
        ],
        compiler_params=pltpu.CompilerParams(vmem_limit_bytes=24 * MIB),
        name="lay",
    )(length, keys.reshape(4096, 128), values.reshape(4096, 128))


def eye_mask(rows):
    row = lax.broadcasted_iota(jnp.int32, (rows, 128), 0)
    lane = lax.broadcasted_iota(jnp.int32, (rows, 128), 1)
    return row, lane


def attend_kernel(length, q0, q1, k_ref, v_ref, *refs, base):
    o_ref, q_s, k_s, v_s, o_s, st_s, q_sem, kv_sem, o_sem, st_sem = refs[-10:]
    core = lax.rem(lax.axis_index("tensor").astype(jnp.int32), 2)

    def fetch_q(j):
        return pltpu.make_async_copy((q0, q1)[j].at[pl.ds(0, 2048), :], q_s.at[j], q_sem.at[j])

    def fetch_kv(head, c):
        rows = pl.ds(c * 1024, 1024)
        return (
            pltpu.make_async_copy(
                k_ref.at[head, rows, :], k_s.at[head, rows, :], kv_sem.at[head, 0, c]
            ),
            pltpu.make_async_copy(
                v_ref.at[head, rows, :], v_s.at[head, rows, pl.ds(0, 128)], kv_sem.at[head, 1, c]
            ),
        )

    def place(j):
        return 2 * (core + j * (1 - 2 * core))

    def send(head, j, half):
        start = pl.multiple_of((2 * (place(j) + half) + head) * 64, 64)
        return pltpu.make_async_copy(
            o_s.at[:, pl.ds(start, 64), :],
            o_ref.at[:, pl.ds(pl.multiple_of(base + start, 16), 64), :],
            o_sem.at[2 * head + j, half],
        )

    for copy in fetch_kv(0, 0) + fetch_kv(0, 1) + (fetch_q(0), fetch_q(1)):
        copy.start()
    for copy in fetch_kv(1, 0) + fetch_kv(1, 1):
        copy.start()
    live = lax.broadcasted_iota(jnp.int32, (2048, 128), 0) < length[0]
    live = jnp.where(live, 1.0, 0.0).astype(BF)
    v_s[0, :, 128:256] = live
    v_s[1, :, 128:256] = live
    for copy in fetch_kv(0, 0) + fetch_kv(0, 1) + (fetch_q(0), fetch_q(1)):
        copy.wait()
    row, lane = eye_mask(64)

    @pl.loop(0, 4)
    def _(step):
        head = step // 2
        j = step % 2

        @pl.when(step == 2)
        def _():
            for copy in fetch_kv(1, 0) + fetch_kv(1, 1):
                copy.wait()

        for s in range(4):
            q = q_s[j, pl.ds(pl.multiple_of(head * 1024 + s * SUB, SUB), SUB), :]
            peak = None
            for b in range(2048 // KEY_BLOCK):
                keys = slice(b * KEY_BLOCK, (b + 1) * KEY_BLOCK)
                scores = dot_nt(q, k_s[head, keys, :])
                top = jnp.ceil(jnp.max(scores, axis=1, keepdims=True) * SCALE)
                new = top if peak is None else jnp.maximum(peak, top)
                weights = jnp.exp2(scores * SCALE - new).astype(BF)
                part = dot_nn(weights, v_s[head, keys, :])
                acc = part if peak is None else acc * jnp.exp2(peak - new) + part
                peak = new
            unit = 2 * (place(j) + s // 2) + head
            for d in range(4):
                dest = 4 * (s % 2) + d
                rows = slice(d * 64, (d + 1) * 64)
                to = pl.ds(pl.multiple_of(unit * 64, 64), 64)
                o_s[dest, to, :] = acc[rows, 0:128].astype(BF)
                pair = jnp.where(
                    lane == row,
                    peak[rows, :],
                    jnp.where(lane == row + 64, acc[rows, 128:256], 0.0),
                )
                st_s[dest, pl.ds(unit, 1), :] = jnp.sum(pair, axis=0, keepdims=True)
        send(head, j, 0).start()
        send(head, j, 1).start()

    for dest in range(8):
        stats = st_s[dest]
        high = stats.astype(BF).astype(F32)
        o_s[dest, 512:528, :] = jnp.concatenate([high, stats - high], axis=0).astype(BF)
    tail = pltpu.make_async_copy(
        o_s.at[:, pl.ds(512, 16), :], o_ref.at[:, pl.ds(base + 512, 16), :], st_sem
    )
    tail.start()
    for head in range(2):
        for j in range(2):
            for half in range(2):
                send(head, j, half).wait()
    tail.wait()


def attend(qs, keys, values, length, before, name):
    any_space = pl.BlockSpec(memory_space=pl.ANY)
    args = [length, *qs, keys, values]
    aliases = {}
    if before is not None:
        aliases = {len(args): 0}
        args.append(before)
    return pl.pallas_call(
        functools.partial(attend_kernel, base=0 if before is None else 528),
        in_specs=[pl.BlockSpec(memory_space=pltpu.SMEM)] + [any_space] * (len(args) - 1),
        out_specs=any_space,
        scratch_shapes=[
            pltpu.VMEM((2, 2048, 128), BF),
            pltpu.VMEM((2, 2048, 128), BF),
            pltpu.VMEM((2, 2048, 256), BF),
            pltpu.VMEM((8, 528, 128), BF),
            pltpu.VMEM((8, 8, 128), F32),
            pltpu.SemaphoreType.DMA((2,)),
            pltpu.SemaphoreType.DMA((2, 2, 2)),
            pltpu.SemaphoreType.DMA((4, 2)),
            pltpu.SemaphoreType.DMA(()),
        ],
        out_shape=jax.ShapeDtypeStruct((8, 1056, 128), BF),
        input_output_aliases=aliases,
        compiler_params=pltpu.CompilerParams(vmem_limit_bytes=40 * MIB),
        cost_estimate=pl.CostEstimate(
            flops=4 * 4096 * 2048 * 128, bytes_accessed=4 * MIB, transcendentals=4096 * 2048
        ),
        name=name,
    )(*args)


def weigh(stats):
    peak = functools.reduce(jnp.maximum, stats)
    factors = [jnp.exp2(s - peak) for s in stats]
    sums = [pltpu.roll(s, 64, 1) for s in stats]
    return peak, factors, sums


def spread(pairs, row, lane):
    hit = (lane == row) | (lane == row + 64)
    return jnp.concatenate([jnp.where(hit, p, 0.0) for p in pairs], axis=1)


def pair_up(first, second, lane):
    return jnp.where(lane[0:1] < 64, first, pltpu.roll(second, 64, 1))


def fold_kernel(in_ref, out_ref, o_ref, sem):
    half = lax.div(lax.axis_index("tensor").astype(jnp.int32), 2)
    halves = (half, 1 - half)
    row, lane = eye_mask(64)
    lane8 = lax.broadcasted_iota(jnp.int32, (8, 128), 1)
    tile = lax.broadcasted_iota(jnp.int32, (16, 128), 0)
    for n in range(2):
        base = 528 * n
        stats = []
        for src in range(8):
            block = in_ref[src, base + 512 : base + 528, :].astype(F32)
            stats.append(block[0:8] + block[8:16])
        peak, factors, sums = weigh(stats)
        factors = [f.astype(BF).astype(F32) for f in factors]
        total = functools.reduce(jnp.add, [f * s for f, s in zip(factors, sums)])
        rolled = [pltpu.roll(f, 64, 1) for f in factors]
        joined = [jnp.where(lane8 < 64, factors[2 * p], rolled[2 * p + 1]) for p in range(4)]
        new = jnp.where(lane8 < 64, peak, pltpu.roll(total, 64, 1))
        high = new.astype(BF).astype(F32)
        low = new - high
        for zl in range(4):
            z = halves[n] * 4 + zl
            value = jnp.zeros((16, 128), F32)
            for head in range(2):
                unit = 2 * zl + head
                mix = spread([x[unit : unit + 1] for x in joined], row, lane).astype(BF)
                at = base + unit * 64
                parts = in_ref[:, at : at + 64, :].reshape(512, 128)
                o_ref[z, head * 64 : head * 64 + 64, :] = dot_nn(mix, parts).astype(BF)
                value = jnp.where(tile == 2 * head, high[unit : unit + 1], value)
                value = jnp.where(tile == 2 * head + 1, low[unit : unit + 1], value)
            o_ref[z, 128:144, :] = value.astype(BF)
            pltpu.make_async_copy(o_ref.at[z], out_ref.at[z], sem.at[4 * n + zl]).start()
    for n in range(2):
        for zl in range(4):
            z = halves[n] * 4 + zl
            pltpu.make_async_copy(o_ref.at[z], out_ref.at[z], sem.at[4 * n + zl]).wait()


def fold(parts):
    return pl.pallas_call(
        fold_kernel,
        in_specs=[pl.BlockSpec(memory_space=pltpu.VMEM)],
        out_specs=pl.BlockSpec(memory_space=pl.ANY),
        out_shape=jax.ShapeDtypeStruct((8, 144, 128), BF),
        scratch_shapes=[pltpu.VMEM((8, 144, 128), BF), pltpu.SemaphoreType.DMA((8,))],
        compiler_params=pltpu.CompilerParams(vmem_limit_bytes=24 * MIB),
        name="fold",
    )(parts)


def prompt_kernel(where, slots, *refs):
    q_refs, kv_refs, o_ref, st_ref = refs[:8], refs[8:12], refs[12], refs[13]
    row, lane = eye_mask(64)
    query = where[1] * 4 + lax.broadcasted_iota(jnp.int32, (64, 64), 0) // 16
    column = lax.broadcasted_iota(jnp.int32, (64, 64), 1)
    mine = where[1] // 16
    for h in range(2):
        q = q_refs[4 * h][...]
        for j in range(1, 4):
            q = jnp.where(slots[j] == mine, q_refs[4 * h + j][...], q)
        scores = []
        for j in range(4):
            part = dot_nt(q, kv_refs[j][h * 128 : h * 128 + 64, :]) * SCALE
            seen = column + slots[j] * 64 <= query
            scores.append(jnp.where(seen, part, -jnp.inf))
        top = functools.reduce(jnp.maximum, [jnp.max(s, axis=1, keepdims=True) for s in scores])
        top = jnp.ceil(top)
        acc = jnp.zeros((64, 128), F32)
        total = jnp.zeros((64, 1), F32)
        for j in range(4):
            weights = jnp.exp2(scores[j] - top).astype(BF)
            total = total + jnp.sum(weights.astype(F32), axis=1, keepdims=True)
            acc = acc + dot_nn(weights, kv_refs[j][h * 128 + 64 : h * 128 + 128, :])
        o_ref[h] = acc.astype(BF)
        pair = jnp.where(lane == row, top, jnp.where(lane == row + 64, total, 0.0))
        st_ref[h] = jnp.broadcast_to(jnp.sum(pair, axis=0, keepdims=True), (8, 128))


def prompt_part(qs, where, slots):
    first = pl.BlockSpec((64, 128), lambda i, w, s: (w[0], 0))
    second = pl.BlockSpec((64, 128), lambda i, w, s: (16 + w[0], 0))
    kv_spec = pl.BlockSpec((256, 128), lambda i, w, s: (8, 0))
    return pl.pallas_call(
        prompt_kernel,
        grid_spec=pltpu.PrefetchScalarGridSpec(
            num_scalar_prefetch=2,
            grid=(1,),
            in_specs=[first] * 4 + [second] * 4 + [kv_spec] * 4,
            out_specs=[
                pl.BlockSpec((2, 64, 128), lambda i, w, s: (0, 0, 0)),
                pl.BlockSpec((2, 8, 128), lambda i, w, s: (0, 0, 0)),
            ],
        ),
        out_shape=[
            jax.ShapeDtypeStruct((2, 64, 128), BF),
            jax.ShapeDtypeStruct((2, 8, 128), F32),
        ],
        compiler_params=pltpu.CompilerParams(vmem_limit_bytes=40 * MIB),
        name="prompt",
    )(where, slots, *qs, *qs, *qs)


def final_kernel(got_ref, po_ref, pst_ref, o_ref):
    row, lane = eye_mask(64)
    for h in range(2):
        stats = []
        for src in range(8):
            block = got_ref[src, 128:144, :].astype(F32)
            stats.append(block[2 * h : 2 * h + 1] + block[2 * h + 1 : 2 * h + 2])
        stats.append(pst_ref[h][0:1])
        peak, factors, sums = weigh(stats)
        total = functools.reduce(jnp.add, [f * s for f, s in zip(factors, sums)])
        inverse = 1.0 / jnp.where(lane[0:1] < 64, total, 1.0)
        factors = [f * inverse for f in factors]
        factors.append(jnp.zeros_like(inverse))
        mix = spread([pair_up(factors[2 * p], factors[2 * p + 1], lane) for p in range(5)], row, lane)
        parts = got_ref[:, h * 64 : h * 64 + 64, :].reshape(512, 128)
        parts = jnp.concatenate([parts, po_ref[h], jnp.zeros((64, 128), BF)], axis=0)
        high = mix.astype(BF)
        low = (mix - high.astype(F32)).astype(BF)
        out = dot_nn(high, parts) + dot_nn(low, parts)
        o_ref[:, h * 16 : h * 16 + 16, :] = out.astype(BF).reshape(4, 16, 128)


def final(got, part_out, part_stats):
    return pl.pallas_call(
        final_kernel,
        out_shape=jax.ShapeDtypeStruct((4, 32, 128), BF),
        compiler_params=pltpu.CompilerParams(vmem_limit_bytes=16 * MIB),
        name="final",
    )(got, part_out, part_stats)


def body(
    queries,
    prompt_keys,
    prompt_values,
    cache_keys,
    cache_values,
    cache_lengths,
    offset,
    prompt_positions,
):
    axes = ("context", "tensor")
    context = lax.axis_index("context").astype(jnp.int32)
    own, swapped, ahead, back = turn(queries, offset, prompt_positions, prompt_keys, prompt_values)
    ahead = lax.ppermute(ahead, axes, shift(1, 0))
    back = lax.ppermute(back, axes, shift(-1, 1))
    swapped = lax.ppermute(swapped, axes, shift(0, 1))
    keys, values = lay(cache_keys, cache_values, cache_lengths)

    plane = [[z * 8 + r for r in range(8)] for z in range(8)]
    column = [[z * 8 + r for z in range(8)] for r in range(8)]

    def swap(parts, groups):
        return lax.all_to_all(
            parts, "context", split_axis=0, concat_axis=0, axis_index_groups=groups, tiled=True
        )

    parts = attend((own, swapped), keys, values, cache_lengths, None, "near")
    parts = attend((ahead, back), keys, values, cache_lengths, parts, "far")
    parts = swap(parts, plane)
    where = jnp.stack([context % 16, context])
    slots = jnp.stack(slots_of())
    part_out, part_stats = prompt_part((own, swapped, ahead, back), where, slots)
    got = swap(fold(parts), column)
    return final(got, part_out, part_stats)


def solution(mesh):
    in_specs = (
        P("tensor", None, None),
        P("tensor", None, None),
        P("tensor", None, None),
        P("context", "tensor", None),
        P("context", "tensor", None),
        P("context"),
        P(),
        P("tensor"),
    )
    out_specs = P("context", "tensor", None)
    return jax.shard_map(body, mesh=mesh, in_specs=in_specs, out_specs=out_specs, check_vma=False)
```

time: 117 us -> 93 us (0.79)
  waiting for transfers between devices: 30.7 us -> 10.1 us
  blocking collectives: 21.9 us -> 35.1 us
  starting transfers between devices: 19.7 us -> 10.9 us
  local copies, waits for them, and re-layouts: 8.82 us -> 1.07 us
  Pallas kernels: 31.4 us -> 33.9 us
  other arithmetic: 2.35 us -> 0.15 us
    ppermute x6 -> x3, waiting for transfers between devices: 21.4 us -> 0.01 us  [the longest x1 0.01 us: body(): swapped = lax.ppermute(swapped, axes, shift(0, 1))]
    all_to_all x1, blocking collectives: 21.9 us -> 35.1 us  [swap(): lax.all_to_all(parts, 'context', split_axis=0, concat_axis=0, axis_index_...]
    unnamed x41 -> x8, local copies, waits for them, and re-layouts: 7.65 us -> 1.07 us
    all_to_all x2 -> x1, starting transfers between devices: 14.5 us -> 8.48 us  [swap(): lax.all_to_all(parts, 'context', split_axis=0, concat_axis=0, axis_index_...]
    ppermute x6 -> x3, starting transfers between devices: 5.15 us -> 2.38 us  [the longest x1 1.65 us: body(): ahead = lax.ppermute(ahead, axes, shift(1, 0))]
    pallas_call x5, Pallas kernels: 29.2 us -> 31.7 us  [the longest x2 24.4 us: attend(): pl.pallas_call(functools.partial(attend_kernel, base=0 if before is None...]
    another operation x2 -> x1, other arithmetic: 1.28 us -> 0.08 us  [body(): slots = jnp.stack(slots_of())]
    all_to_all x2 -> x1, waiting for transfers between devices: 9.23 us -> 10.1 us  [swap(): lax.all_to_all(parts, 'context', split_axis=0, concat_axis=0, axis_index_...]
  transfers between devices with their start and end apart: 8 -> 4, of which waited for: 5 -> 1; matrix products, arithmetic and copies ran while one was open for 3% -> 0% of each run, Pallas kernels for 13% -> 16%
where the time goes in v2:
time: 93 us; the launch traced here: 92.7 us
  blocking collectives  35.1 us (38%)
  Pallas kernels  33.9 us (36%)
  starting transfers between devices  10.9 us (12%)
  waiting for transfers between devices  10.1 us (11%)
  between operations  1.55 us (2%)
  local copies, waits for them, and re-layouts  1.07 us (1%)
    all_to_all x1, blocking collectives, swap(): lax.all_to_all(parts, 'context', split_axis=0, concat_axis=0, axis_index_...  35.1 us
    pallas_call x2, Pallas kernels, attend(): pl.pallas_call(functools.partial(attend_kernel, base=0 if before is None...  24.4 us
    all_to_all x1, waiting for transfers between devices, swap(): lax.all_to_all(parts, 'context', split_axis=0, concat_axis=0, axis_index_...  10.1 us
    all_to_all x1, starting transfers between devices, swap(): lax.all_to_all(parts, 'context', split_axis=0, concat_axis=0, axis_index_...  8.48 us
    pallas_call x1, Pallas kernels, turn(): pl.pallas_call(turn_kernel, in_specs=[pl.BlockSpec(memory_space=pltpu.SME...  4.79 us
  transfers between devices with their start and end apart: 4, of which 1 were waited for; matrix products, arithmetic and copies ran while one was open for 0% of the time, Pallas kernels for 16%

profile of v2, /device:TPU:8, one launch (start us, length us, event | category | flops | bytes accessed | tf_op | source)
XLA Modules:
  0.0 92.7 jit_solution(14407476052456942784)
XLA Ops:
  0.0 0.0 copy-start.3
  0.0 0.0 copy-start.2
  0.8 4.8 %turn.1 = (bf16[2304,128]{1,0:T(8,128)(2,1)}, bf16[2304,128]{1,0:T(8,128)(2,1)}, bf16[2304,128]{1,0:T(8,128)(2,1)}, bf16[2304,128]{1,0:T(8,128)(2,1)}) custom-call(s32[1]{0:T(128)S(6)} %copy.13.offset, s32[1,64]{1,0:T(1,128)} %bitcast.11, f32[1,128]{1,0:T(1,128)} %constant.32.clone.freq_ref, bf16[64,8,128]{2,1,0:T(8,128)(2,1)} %k_ref.1, ...), custom_call_target="tpu_custom_call" | custom-call | tf_op jit(solution)/shard_map/turn/pallas_call | solution.py:109
  5.6 0.1 collective-permute-start.2
  5.7 1.7 %collective-permute-start = (bf16[2304,128]{1,0:T(8,128)(2,1)}, bf16[2304,128]{1,0:T(8,128)(2,1)S(1)}, u32[]{:S(2)}, u32[]{:S(2)}) collective-permute-start(bf16[2304,128]{1,0:T(8,128)(2,1)} %get-tuple-element.13), channel_id=1, source_target_pairs={{0,2},{1,3},{2,4},{3,5},{4,6},{5,7},{6,0},{7,1},{8,10},{9,11},{10,... | collective-permute-start | bytes 1769480 | tf_op jit(solution)/shard_map/ppermute | solution.py:470
  7.4 0.6 collective-permute-start.1
  8.6 0.0 copy-done.3
  8.7 0.0 copy-done.2
  8.7 1.3 %lay.1 = (bf16[2,2048,128]{2,1,0:T(8,128)(2,1)S(1)}, bf16[2,2048,128]{2,1,0:T(8,128)(2,1)S(1)}) custom-call(s32[1]{0:T(128)S(6)} %copy.12.length, bf16[4096,128]{1,0:T(8,128)(2,1)S(1)} %bitcast.9, bf16[4096,128]{1,0:T(8,128)(2,1)S(1)} %bitcast.10), custom_call_target="tpu_custom_call" | custom-call | tf_op jit(solution)/shard_map/lay/pallas_call | solution.py:159
  10.0 0.0 collective-permute-done.2.q1.refs_1_.refs_5_.refs_9_
  10.0 0.0 copy-start
  10.0 1.1 %copy-done = bf16[2304,128]{1,0:T(8,128)(2,1)S(1)} copy-done((bf16[2304,128]{1,0:T(8,128)(2,1)S(1)}, bf16[2304,128]{1,0:T(8,128)(2,1)}, u32[]{:S(2)}) %copy-start) | copy-done | bytes 589848
  11.1 12.2 %near.1.refs_0_ = bf16[8,1056,128]{2,1,0:T(8,128)(2,1)S(1)} custom-call(s32[1]{0:T(128)S(6)} %copy.12.length, bf16[2304,128]{1,0:T(8,128)(2,1)S(1)} %copy-done, bf16[2304,128]{1,0:T(8,128)(2,1)S(1)} %collective-permute-done.2.q1.refs_1_.refs_5_.refs_9_, bf16[2,2048,128]{2,1,0:T(8,128)(2,1)S(1)} %get-tuple-element.15.k_ref, ...), custom_call_target="tpu_custom_call" | custom-call | flops 4294967296 | bytes 4194304 | tf_op jit(solution)/shard_map/near/pallas_call | solution.py:282
  23.3 0.0 collective-permute-done.q0.refs_2_.refs_6_.refs_10_
  23.3 0.0 collective-permute-done.1.q1.refs_3_.refs_7_.refs_11_
  23.3 12.2 %far.1 = bf16[8,1056,128]{2,1,0:T(8,128)(2,1)S(1)} custom-call(s32[1]{0:T(128)S(6)} %copy.12.length, bf16[2304,128]{1,0:T(8,128)(2,1)S(1)} %collective-permute-done.q0.refs_2_.refs_6_.refs_10_, bf16[2304,128]{1,0:T(8,128)(2,1)S(1)} %collective-permute-done.1.q1.refs_3_.refs_7_.refs_11_, ...), custom_call_target="tpu_custom_call", output_to_operand_aliasing={{}: (5, {})} | custom-call | flops 4294967296 | bytes 4194304 | tf_op jit(solution)/shard_map/far/pallas_call | solution.py:282
  35.5 35.1 %all_to_all.10.in_ref = bf16[8,1056,128]{2,1,0:T(8,128)(2,1)S(1)} all-to-all(bf16[8,1056,128]{2,1,0:T(8,128)(2,1)S(1)} %far.1), channel_id=1, replica_groups={{0,4,8,12,16,20,24,28},{32,36,40,44,48,52,56,60},{64,68,72,76,80,84,88,..., dimensions={0} | all-to-all | bytes 4325376 | tf_op jit(solution)/shard_map/all_to_all | solution.py:479
  70.6 0.0 copy-start.1
  70.6 1.2 %fold.1 = bf16[8,144,128]{2,1,0:T(8,128)(2,1)} custom-call(bf16[8,1056,128]{2,1,0:T(8,128)(2,1)S(1)} %all_to_all.10.in_ref), custom_call_target="tpu_custom_call" | custom-call | tf_op jit(solution)/shard_map/fold/pallas_call | solution.py:363
  71.8 8.5 %all-to-all-start.1 = ((bf16[8,144,128]{2,1,0:T(8,128)(2,1)}), bf16[8,144,128]{2,1,0:T(8,128)(2,1)S(1)}, u32[]{:S(2)}, u32[]{:S(2)}) async-start(bf16[8,144,128]{2,1,0:T(8,128)(2,1)} %fold.1), calls=%async_computation.1 | async-start | bytes 589824 | tf_op jit(solution)/shard_map/all_to_all | solution.py:479
  80.3 0.1 pad_add_fusion.where
  80.4 0.1 pad_add_fusion.1.slots
  80.4 0.0 copy-done.1
  80.4 1.2 %prompt.1 = (bf16[2,64,128]{2,1,0:T(8,128)(2,1)S(1)}, f32[2,8,128]{2,1,0:T(8,128)S(1)}) custom-call(s32[2]{0:T(128)S(1)} %pad_add_fusion.where, s32[4]{0:T(128)S(1)} %pad_add_fusion.1.slots, bf16[2304,128]{1,0:T(8,128)(2,1)S(1)} %copy-done.1, bf16[2304,128]{1,0:T(8,128)(2,1)S(1)} %collective-permute-done.2.q1.refs_1_.refs_5_.refs_9_, ...), custom_call_target="tpu_custom_call" | custom-call | tf_op jit(solution)/shard_map/prompt/pallas_call | solution.py:406
  81.6 10.1 %all-to-all-done.1.got_ref = bf16[8,144,128]{2,1,0:T(8,128)(2,1)S(1)} async-done(((bf16[8,144,128]{2,1,0:T(8,128)(2,1)}), bf16[8,144,128]{2,1,0:T(8,128)(2,1)S(1)}, u32[]{:S(2)}, u32[]{:S(2)}) %all-to-all-start.1) | async-done | bytes 294944 | tf_op jit(solution)/shard_map/all_to_all | solution.py:479
  91.7 1.0 %final.1 = bf16[4,32,128]{2,1,0:T(8,128)(2,1)} custom-call(bf16[8,144,128]{2,1,0:T(8,128)(2,1)S(1)} %all-to-all-done.1.got_ref, bf16[2,64,128]{2,1,0:T(8,128)(2,1)S(1)} %get-tuple-element.19.po_ref, f32[2,8,128]{2,1,0:T(8,128)S(1)} %get-tuple-element.20.pst_ref), custom_call_target="tpu_custom_call" | custom-call | tf_op jit(solution)/shard_map/final/pallas_call | solution.py:449
Async XLA Ops:
  0.0 8.6 %copy-start.3 = (bf16[2048,2,128]{2,1,0:T(2,128)(2,1)S(1)}, bf16[2048,2,128]{2,1,0:T(2,128)(2,1)}, u32[]{:S(2)}) copy-start(bf16[2048,2,128]{2,1,0:T(2,128)(2,1)} %param.13) | copy-start | bytes 3145732
  0.0 8.7 %copy-start.2 = (bf16[2048,2,128]{2,1,0:T(2,128)(2,1)S(1)}, bf16[2048,2,128]{2,1,0:T(2,128)(2,1)}, u32[]{:S(2)}) copy-start(bf16[2048,2,128]{2,1,0:T(2,128)(2,1)} %param.12) | copy-start | bytes 3145732
  5.6 4.4 %collective-permute-start.2 = (bf16[2304,128]{1,0:T(8,128)(2,1)}, bf16[2304,128]{1,0:T(8,128)(2,1)S(1)}, u32[]{:S(2)}, u32[]{:S(2)}) collective-permute-start(bf16[2304,128]{1,0:T(8,128)(2,1)} %get-tuple-element.18), channel_id=1, source_target_pairs={{0,1},{1,0},{2,3},{3,2},{4,5},{5,4},{6,7},{7,6},{8,9},{9,8},{10,11... | collective-permute-start | bytes 1769480 | tf_op jit(solution)/shard_map/ppermute | solution.py:472
  5.7 17.6 %collective-permute-start = (bf16[2304,128]{1,0:T(8,128)(2,1)}, bf16[2304,128]{1,0:T(8,128)(2,1)S(1)}, u32[]{:S(2)}, u32[]{:S(2)}) collective-permute-start(bf16[2304,128]{1,0:T(8,128)(2,1)} %get-tuple-element.13), channel_id=1, source_target_pairs={{0,2},{1,3},{2,4},{3,5},{4,6},{5,7},{6,0},{7,1},{8,10},{9,11},{10,... | collective-permute-start | bytes 1769480 | tf_op jit(solution)/shard_map/ppermute | solution.py:470
  7.4 15.9 %collective-permute-start.1 = (bf16[2304,128]{1,0:T(8,128)(2,1)}, bf16[2304,128]{1,0:T(8,128)(2,1)S(1)}, u32[]{:S(2)}, u32[]{:S(2)}) collective-permute-start(bf16[2304,128]{1,0:T(8,128)(2,1)} %get-tuple-element.14), channel_id=1, source_target_pairs={{0,7},{1,6},{2,1},{3,0},{4,3},{5,2},{6,5},{7,4},{8,15},{9,14},{10,... | collective-permute-start | bytes 1769480 | tf_op jit(solution)/shard_map/ppermute | solution.py:471
  10.0 1.1 %copy-start = (bf16[2304,128]{1,0:T(8,128)(2,1)S(1)}, bf16[2304,128]{1,0:T(8,128)(2,1)}, u32[]{:S(2)}) copy-start(bf16[2304,128]{1,0:T(8,128)(2,1)} %get-tuple-element.17.q0.refs_0_.refs_4_.refs_8_) | copy-start | bytes 1769476
  70.6 9.8 %copy-start.1 = (bf16[2304,128]{1,0:T(8,128)(2,1)S(1)}, bf16[2304,128]{1,0:T(8,128)(2,1)}, u32[]{:S(2)}) copy-start(bf16[2304,128]{1,0:T(8,128)(2,1)} %get-tuple-element.17.q0.refs_0_.refs_4_.refs_8_) | copy-start | bytes 1769476
  71.8 19.9 %all-to-all-start.1 = ((bf16[8,144,128]{2,1,0:T(8,128)(2,1)}), bf16[8,144,128]{2,1,0:T(8,128)(2,1)S(1)}, u32[]{:S(2)}, u32[]{:S(2)}) async-start(bf16[8,144,128]{2,1,0:T(8,128)(2,1)} %fold.1), calls=%async_computation.1 | async-start | bytes 589824 | tf_op jit(solution)/shard_map/all_to_all | solution.py:479

commit v3 on v2

--- a/solution.py
+++ b/solution.py
@@ -66,11 +66,17 @@
     column = lax.broadcasted_iota(jnp.int32, (64, 64), 1)
     position = (pos_ref[...] + offset[0]).astype(F32)
     position = jnp.sum(jnp.where(row == column, position, 0.0), axis=1, keepdims=True)
-    angle = position * freq_ref[...]
+    left = lax.broadcasted_iota(jnp.int32, (32, 128), 1) < 64
+    angle = jnp.where(left, position[0:32], position[32:64]) * freq_ref[...]
+    both = []
+    for value in (jnp.cos(angle), jnp.sin(angle)):
+        moved = pltpu.roll(value, 64, 1)
+        above = jnp.where(left, value, moved)
+        below = jnp.where(left, moved, value)
+        both.append(jnp.concatenate([above, below], axis=0))
     lane = lax.broadcasted_iota(jnp.int32, (64, 128), 1)
-    cosine = jnp.cos(angle)
-    sine = jnp.sin(angle)
-    sine = jnp.where(lane < 64, -sine, sine)
+    cosine = both[0]
+    sine = jnp.where(lane < 64, -both[1], both[1])
     cos_s[...] = cosine
     sin_s[...] = sine
     wide = k_ref[...].astype(F32)
@@ -80,7 +86,7 @@
     for j in order:
         fetch(j).wait()
 
-        @pl.loop(0, 4)
+        @pl.loop(0, 4, unroll=True)
         def _(i):
             rows = pl.ds(pl.multiple_of(i * 16, 16), 16)
             cosine = cos_s[rows, :][:, None, :]
@@ -125,49 +131,33 @@
     )(offset, positions.reshape(1, 64), freq, keys, values, queries)
 
 
-def lay_kernel(length, k_ref, v_ref, ko_ref, vo_ref, in_s, wide_s, out_s, in_sem, out_sem):
-    refs, outs = (k_ref, v_ref), (ko_ref, vo_ref)
-
-    def fetch(n, c):
-        rows = pl.ds(c * 1024, 1024)
-        return pltpu.make_async_copy(refs[n].at[rows, :], in_s.at[n, rows, :], in_sem.at[n, c])
-
-    def send(n, c):
-        rows = pl.ds(c * 512, 512)
-        return pltpu.make_async_copy(
-            out_s.at[n, :, rows, :], outs[n].at[:, rows, :], out_sem.at[n, c]
-        )
-
-    parts = [(n, c) for c in range(4) for n in range(2)]
-    for n, c in parts:
-        fetch(n, c).start()
-    for n, c in parts:
-        fetch(n, c).wait()
+def lay_kernel(length, k_ref, v_ref, ko_ref, vo_ref, wide_s):
+    for c in range(4):
         live = lax.broadcasted_iota(jnp.int32, (512, 128), 0) + c * 512 < length[0]
-        wide_s[n] = in_s[n, c * 1024 : c * 1024 + 1024, :].astype(F32)
-        first = in_s[n, 0:16, :].astype(F32)
+        rows = slice(c * 512, c * 512 + 512)
+        wide_s[0] = k_ref[c * 1024 : c * 1024 + 1024, :].astype(F32)
+        wide_s[1] = v_ref[c * 1024 : c * 1024 + 1024, :].astype(F32)
+        first = k_ref[0:16, :].astype(F32)
+        one = jnp.where(live, 1.0, 0.0).astype(BF)
         for head in range(2):
-            value = wide_s[n, pl.ds(head, 512, 2), :]
-            dead = first[head : head + 1, :] if n == 0 else 0.0
-            out_s[n, head, c * 512 : c * 512 + 512, :] = jnp.where(live, value, dead).astype(BF)
-        send(n, c).start()
-    for n, c in parts:
-        send(n, c).wait()
+            keys = wide_s[0, pl.ds(head, 512, 2), :]
+            values = wide_s[1, pl.ds(head, 512, 2), :]
+            ko_ref[head, rows, :] = jnp.where(live, keys, first[head : head + 1, :]).astype(BF)
+            vo_ref[head, rows, 0:128] = jnp.where(live, values, 0.0).astype(BF)
+            vo_ref[head, rows, 128:256] = one
 
 
 def lay(keys, values, length):
+    vmem = pl.BlockSpec(memory_space=pltpu.VMEM)
     return pl.pallas_call(
         lay_kernel,
-        in_specs=[pl.BlockSpec(memory_space=pltpu.SMEM)] + [pl.BlockSpec(memory_space=pl.ANY)] * 2,
-        out_specs=[pl.BlockSpec(memory_space=pl.ANY)] * 2,
-        out_shape=[jax.ShapeDtypeStruct((2, 2048, 128), BF)] * 2,
-        scratch_shapes=[
-            pltpu.VMEM((2, 4096, 128), BF),
-            pltpu.VMEM((2, 1024, 128), F32),
-            pltpu.VMEM((2, 2, 2048, 128), BF),
-            pltpu.SemaphoreType.DMA((2, 4)),
-            pltpu.SemaphoreType.DMA((2, 4)),
+        in_specs=[pl.BlockSpec(memory_space=pltpu.SMEM), vmem, vmem],
+        out_specs=[vmem, vmem],
+        out_shape=[
+            jax.ShapeDtypeStruct((2, 2048, 128), BF),
+            jax.ShapeDtypeStruct((2, 2048, 256), BF),
         ],
+        scratch_shapes=[pltpu.VMEM((2, 1024, 128), F32)],
         compiler_params=pltpu.CompilerParams(vmem_limit_bytes=24 * MIB),
         name="lay",
     )(length, keys.reshape(4096, 128), values.reshape(4096, 128))
@@ -179,23 +169,9 @@
     return row, lane
 
 
-def attend_kernel(length, q0, q1, k_ref, v_ref, *refs, base):
-    o_ref, q_s, k_s, v_s, o_s, st_s, q_sem, kv_sem, o_sem, st_sem = refs[-10:]
+def attend_kernel(q0, q1, k_ref, v_ref, *refs, base):
+    o_ref, q_s, o_s, st_s, o_sem, st_sem = refs[-6:]
     core = lax.rem(lax.axis_index("tensor").astype(jnp.int32), 2)
-
-    def fetch_q(j):
-        return pltpu.make_async_copy((q0, q1)[j].at[pl.ds(0, 2048), :], q_s.at[j], q_sem.at[j])
-
-    def fetch_kv(head, c):
-        rows = pl.ds(c * 1024, 1024)
-        return (
-            pltpu.make_async_copy(
-                k_ref.at[head, rows, :], k_s.at[head, rows, :], kv_sem.at[head, 0, c]
-            ),
-            pltpu.make_async_copy(
-                v_ref.at[head, rows, :], v_s.at[head, rows, pl.ds(0, 128)], kv_sem.at[head, 1, c]
-            ),
-        )
 
     def place(j):
         return 2 * (core + j * (1 - 2 * core))
@@ -208,16 +184,6 @@
             o_sem.at[2 * head + j, half],
         )
 
-    for copy in fetch_kv(0, 0) + fetch_kv(0, 1) + (fetch_q(0), fetch_q(1)):
-        copy.start()
-    for copy in fetch_kv(1, 0) + fetch_kv(1, 1):
-        copy.start()
-    live = lax.broadcasted_iota(jnp.int32, (2048, 128), 0) < length[0]
-    live = jnp.where(live, 1.0, 0.0).astype(BF)
-    v_s[0, :, 128:256] = live
-    v_s[1, :, 128:256] = live
-    for copy in fetch_kv(0, 0) + fetch_kv(0, 1) + (fetch_q(0), fetch_q(1)):
-        copy.wait()
     row, lane = eye_mask(64)
 
     @pl.loop(0, 4)
@@ -225,21 +191,22 @@
         head = step // 2
         j = step % 2
 
-        @pl.when(step == 2)
-        def _():
-            for copy in fetch_kv(1, 0) + fetch_kv(1, 1):
-                copy.wait()
+        for n, ref in enumerate((q0, q1)):
+
+            @pl.when(j == n)
+            def _():
+                q_s[...] = ref[pl.ds(pl.multiple_of(head * 1024, 1024), 1024), :]
 
         for s in range(4):
-            q = q_s[j, pl.ds(pl.multiple_of(head * 1024 + s * SUB, SUB), SUB), :]
+            q = q_s[s * SUB : (s + 1) * SUB, :]
             peak = None
             for b in range(2048 // KEY_BLOCK):
                 keys = slice(b * KEY_BLOCK, (b + 1) * KEY_BLOCK)
-                scores = dot_nt(q, k_s[head, keys, :])
+                scores = dot_nt(q, k_ref[head, keys, :])
                 top = jnp.ceil(jnp.max(scores, axis=1, keepdims=True) * SCALE)
                 new = top if peak is None else jnp.maximum(peak, top)
                 weights = jnp.exp2(scores * SCALE - new).astype(BF)
-                part = dot_nn(weights, v_s[head, keys, :])
+                part = dot_nn(weights, v_ref[head, keys, :])
                 acc = part if peak is None else acc * jnp.exp2(peak - new) + part
                 peak = new
             unit = 2 * (place(j) + s // 2) + head
@@ -272,25 +239,21 @@
     tail.wait()
 
 
-def attend(qs, keys, values, length, before, name):
+def attend(qs, keys, values, before, name):
     any_space = pl.BlockSpec(memory_space=pl.ANY)
-    args = [length, *qs, keys, values]
+    args = [*qs, keys, values]
     aliases = {}
     if before is not None:
         aliases = {len(args): 0}
         args.append(before)
     return pl.pallas_call(
         functools.partial(attend_kernel, base=0 if before is None else 528),
-        in_specs=[pl.BlockSpec(memory_space=pltpu.SMEM)] + [any_space] * (len(args) - 1),
+        in_specs=[pl.BlockSpec(memory_space=pltpu.VMEM)] * 4 + [any_space] * (len(args) - 4),
         out_specs=any_space,
         scratch_shapes=[
-            pltpu.VMEM((2, 2048, 128), BF),
-            pltpu.VMEM((2, 2048, 128), BF),
-            pltpu.VMEM((2, 2048, 256), BF),
+            pltpu.VMEM((1024, 128), BF),
             pltpu.VMEM((8, 528, 128), BF),
             pltpu.VMEM((8, 8, 128), F32),
-            pltpu.SemaphoreType.DMA((2,)),
-            pltpu.SemaphoreType.DMA((2, 2, 2)),
             pltpu.SemaphoreType.DMA((4, 2)),
             pltpu.SemaphoreType.DMA(()),
         ],
@@ -480,8 +443,8 @@
             parts, "context", split_axis=0, concat_axis=0, axis_index_groups=groups, tiled=True
         )
 
-    parts = attend((own, swapped), keys, values, cache_lengths, None, "near")
-    parts = attend((ahead, back), keys, values, cache_lengths, parts, "far")
+    parts = attend((own, swapped), keys, values, None, "near")
+    parts = attend((ahead, back), keys, values, parts, "far")
     parts = swap(parts, plane)
     where = jnp.stack([context % 16, context])
     slots = jnp.stack(slots_of())

time: 93 us -> 91.3 us (0.982)
  Pallas kernels: 33.9 us -> 31.8 us
    pallas_call x2, Pallas kernels: 24.4 us -> 23.4 us  [attend(): pl.pallas_call(functools.partial(attend_kernel, base=0 if before is None...]
  transfers between devices with their start and end apart: 4 -> 4, of which waited for: 1 -> 2; matrix products, arithmetic and copies ran while one was open for 0% -> 0% of each run, Pallas kernels for 16% -> 15%
where the time goes in v3:
time: 91.3 us; the launch traced here: 91 us
  blocking collectives  35.2 us (39%)
  Pallas kernels  31.8 us (35%)
  starting transfers between devices  10.9 us (12%)
  waiting for transfers between devices  10.4 us (11%)
  between operations  1.54 us (2%)
  local copies, waits for them, and re-layouts  1.07 us (1%)
    all_to_all x1, blocking collectives, swap(): lax.all_to_all(parts, 'context', split_axis=0, concat_axis=0, axis_index_...  35.2 us
    pallas_call x2, Pallas kernels, attend(): pl.pallas_call(functools.partial(attend_kernel, base=0 if before is None...  23.4 us
    all_to_all x1, waiting for transfers between devices, swap(): lax.all_to_all(parts, 'context', split_axis=0, concat_axis=0, axis_index_...  10.1 us
    all_to_all x1, starting transfers between devices, swap(): lax.all_to_all(parts, 'context', split_axis=0, concat_axis=0, axis_index_...  8.48 us
    pallas_call x1, Pallas kernels, turn(): pl.pallas_call(turn_kernel, in_specs=[pl.BlockSpec(memory_space=pltpu.SME...  3.92 us
  transfers between devices with their start and end apart: 4, of which 2 were waited for; matrix products, arithmetic and copies ran while one was open for 0% of the time, Pallas kernels for 15%

profile of v3, /device:TPU:8, one launch (start us, length us, event | category | flops | bytes accessed | tf_op | source)
XLA Modules:
  0.0 91.0 jit_solution(14211735727912733203)
XLA Ops:
  0.0 0.0 copy-start.3
  0.0 0.0 copy-start.2
  0.8 3.9 %turn.1 = (bf16[2304,128]{1,0:T(8,128)(2,1)}, bf16[2304,128]{1,0:T(8,128)(2,1)}, bf16[2304,128]{1,0:T(8,128)(2,1)}, bf16[2304,128]{1,0:T(8,128)(2,1)}) custom-call(s32[1]{0:T(128)S(6)} %copy.13.offset, s32[1,64]{1,0:T(1,128)} %bitcast.11, f32[1,128]{1,0:T(1,128)} %constant.32.clone.freq_ref, bf16[64,8,128]{2,1,0:T(8,128)(2,1)} %k_ref.1, ...), custom_call_target="tpu_custom_call" | custom-call | tf_op jit(solution)/shard_map/turn/pallas_call | solution.py:115
  4.7 0.1 collective-permute-start.2
  4.8 1.7 %collective-permute-start = (bf16[2304,128]{1,0:T(8,128)(2,1)}, bf16[2304,128]{1,0:T(8,128)(2,1)S(1)}, u32[]{:S(2)}, u32[]{:S(2)}) collective-permute-start(bf16[2304,128]{1,0:T(8,128)(2,1)} %get-tuple-element.13), channel_id=1, source_target_pairs={{0,2},{1,3},{2,4},{3,5},{4,6},{5,7},{6,0},{7,1},{8,10},{9,11},{10,... | collective-permute-start | bytes 1769480 | tf_op jit(solution)/shard_map/ppermute | solution.py:433
  6.5 0.6 collective-permute-start.1
  7.8 0.0 copy-done.3
  7.8 0.0 copy-done.2
  7.8 1.1 %lay.1 = (bf16[2,2048,128]{2,1,0:T(8,128)(2,1)S(1)}, bf16[2,2048,256]{2,1,0:T(8,128)(2,1)S(1)}) custom-call(s32[1]{0:T(128)S(6)} %copy.12.length, bf16[4096,128]{1,0:T(8,128)(2,1)S(1)} %bitcast.9, bf16[4096,128]{1,0:T(8,128)(2,1)S(1)} %bitcast.10), custom_call_target="tpu_custom_call" | custom-call | tf_op jit(solution)/shard_map/lay/pallas_call | solution.py:152
  8.9 0.0 collective-permute-done.2.q1.refs_1_.refs_5_.refs_9_
  9.0 0.0 copy-start
  9.0 1.1 %copy-done = bf16[2304,128]{1,0:T(8,128)(2,1)S(1)} copy-done((bf16[2304,128]{1,0:T(8,128)(2,1)S(1)}, bf16[2304,128]{1,0:T(8,128)(2,1)}, u32[]{:S(2)}) %copy-start) | copy-done | bytes 589848
  10.0 11.7 %near.1.refs_0_ = bf16[8,1056,128]{2,1,0:T(8,128)(2,1)S(1)} custom-call(bf16[2304,128]{1,0:T(8,128)(2,1)S(1)} %copy-done, bf16[2304,128]{1,0:T(8,128)(2,1)S(1)} %collective-permute-done.2.q1.refs_1_.refs_5_.refs_9_, bf16[2,2048,128]{2,1,0:T(8,128)(2,1)S(1)} %get-tuple-element.15.k_ref, bf16[2,2048,256]{2,1,0:T(8,128)(2,1)S(1)} %get-tuple-element.16.v_ref), custom_call_target="tpu_custom_call" | custom-call | flops 4294967296 | bytes 4194304 | tf_op jit(solution)/shard_map/near/pallas_call | solution.py:249
  21.7 0.0 collective-permute-done.q0.refs_2_.refs_6_.refs_10_
  21.7 0.3 collective-permute-done.1.q1.refs_3_.refs_7_.refs_11_
  22.0 11.7 %far.1 = bf16[8,1056,128]{2,1,0:T(8,128)(2,1)S(1)} custom-call(bf16[2304,128]{1,0:T(8,128)(2,1)S(1)} %collective-permute-done.q0.refs_2_.refs_6_.refs_10_, bf16[2304,128]{1,0:T(8,128)(2,1)S(1)} %collective-permute-done.1.q1.refs_3_.refs_7_.refs_11_, bf16[2,2048,128]{2,1,0:T(8,128)(2,1)S(1)} %get-tuple-element.15.k_ref, ...), custom_call_target="tpu_custom_call", output_to_operand_aliasing={{}: (4, {})} | custom-call | flops 4294967296 | bytes 4194304 | tf_op jit(solution)/shard_map/far/pallas_call | solution.py:249
  33.7 35.2 %all_to_all.10.in_ref = bf16[8,1056,128]{2,1,0:T(8,128)(2,1)S(1)} all-to-all(bf16[8,1056,128]{2,1,0:T(8,128)(2,1)S(1)} %far.1), channel_id=1, replica_groups={{0,4,8,12,16,20,24,28},{32,36,40,44,48,52,56,60},{64,68,72,76,80,84,88,..., dimensions={0} | all-to-all | bytes 4325376 | tf_op jit(solution)/shard_map/all_to_all | solution.py:442
  68.9 0.0 copy-start.1
  68.9 1.2 %fold.1 = bf16[8,144,128]{2,1,0:T(8,128)(2,1)} custom-call(bf16[8,1056,128]{2,1,0:T(8,128)(2,1)S(1)} %all_to_all.10.in_ref), custom_call_target="tpu_custom_call" | custom-call | tf_op jit(solution)/shard_map/fold/pallas_call | solution.py:326
  70.1 8.5 %all-to-all-start.1 = ((bf16[8,144,128]{2,1,0:T(8,128)(2,1)}), bf16[8,144,128]{2,1,0:T(8,128)(2,1)S(1)}, u32[]{:S(2)}, u32[]{:S(2)}) async-start(bf16[8,144,128]{2,1,0:T(8,128)(2,1)} %fold.1), calls=%async_computation.1 | async-start | bytes 589824 | tf_op jit(solution)/shard_map/all_to_all | solution.py:442
  78.5 0.1 pad_add_fusion.where
  78.6 0.1 pad_add_fusion.1.slots
  78.7 0.0 copy-done.1
  78.7 1.2 %prompt.1 = (bf16[2,64,128]{2,1,0:T(8,128)(2,1)S(1)}, f32[2,8,128]{2,1,0:T(8,128)S(1)}) custom-call(s32[2]{0:T(128)S(1)} %pad_add_fusion.where, s32[4]{0:T(128)S(1)} %pad_add_fusion.1.slots, bf16[2304,128]{1,0:T(8,128)(2,1)S(1)} %copy-done.1, bf16[2304,128]{1,0:T(8,128)(2,1)S(1)} %collective-permute-done.2.q1.refs_1_.refs_5_.refs_9_, ...), custom_call_target="tpu_custom_call" | custom-call | tf_op jit(solution)/shard_map/prompt/pallas_call | solution.py:369
  79.9 10.1 %all-to-all-done.1.got_ref = bf16[8,144,128]{2,1,0:T(8,128)(2,1)S(1)} async-done(((bf16[8,144,128]{2,1,0:T(8,128)(2,1)}), bf16[8,144,128]{2,1,0:T(8,128)(2,1)S(1)}, u32[]{:S(2)}, u32[]{:S(2)}) %all-to-all-start.1) | async-done | bytes 294944 | tf_op jit(solution)/shard_map/all_to_all | solution.py:442
  90.0 1.0 %final.1 = bf16[4,32,128]{2,1,0:T(8,128)(2,1)} custom-call(bf16[8,144,128]{2,1,0:T(8,128)(2,1)S(1)} %all-to-all-done.1.got_ref, bf16[2,64,128]{2,1,0:T(8,128)(2,1)S(1)} %get-tuple-element.19.po_ref, f32[2,8,128]{2,1,0:T(8,128)S(1)} %get-tuple-element.20.pst_ref), custom_call_target="tpu_custom_call" | custom-call | tf_op jit(solution)/shard_map/final/pallas_call | solution.py:412
Async XLA Ops:
  0.0 7.8 %copy-start.3 = (bf16[2048,2,128]{2,1,0:T(2,128)(2,1)S(1)}, bf16[2048,2,128]{2,1,0:T(2,128)(2,1)}, u32[]{:S(2)}) copy-start(bf16[2048,2,128]{2,1,0:T(2,128)(2,1)} %param.13) | copy-start | bytes 3145732
  0.0 7.8 %copy-start.2 = (bf16[2048,2,128]{2,1,0:T(2,128)(2,1)S(1)}, bf16[2048,2,128]{2,1,0:T(2,128)(2,1)}, u32[]{:S(2)}) copy-start(bf16[2048,2,128]{2,1,0:T(2,128)(2,1)} %param.12) | copy-start | bytes 3145732
  4.7 4.2 %collective-permute-start.2 = (bf16[2304,128]{1,0:T(8,128)(2,1)}, bf16[2304,128]{1,0:T(8,128)(2,1)S(1)}, u32[]{:S(2)}, u32[]{:S(2)}) collective-permute-start(bf16[2304,128]{1,0:T(8,128)(2,1)} %get-tuple-element.18), channel_id=1, source_target_pairs={{0,1},{1,0},{2,3},{3,2},{4,5},{5,4},{6,7},{7,6},{8,9},{9,8},{10,11... | collective-permute-start | bytes 1769480 | tf_op jit(solution)/shard_map/ppermute | solution.py:435
  4.8 16.9 %collective-permute-start = (bf16[2304,128]{1,0:T(8,128)(2,1)}, bf16[2304,128]{1,0:T(8,128)(2,1)S(1)}, u32[]{:S(2)}, u32[]{:S(2)}) collective-permute-start(bf16[2304,128]{1,0:T(8,128)(2,1)} %get-tuple-element.13), channel_id=1, source_target_pairs={{0,2},{1,3},{2,4},{3,5},{4,6},{5,7},{6,0},{7,1},{8,10},{9,11},{10,... | collective-permute-start | bytes 1769480 | tf_op jit(solution)/shard_map/ppermute | solution.py:433
  6.5 15.5 %collective-permute-start.1 = (bf16[2304,128]{1,0:T(8,128)(2,1)}, bf16[2304,128]{1,0:T(8,128)(2,1)S(1)}, u32[]{:S(2)}, u32[]{:S(2)}) collective-permute-start(bf16[2304,128]{1,0:T(8,128)(2,1)} %get-tuple-element.14), channel_id=1, source_target_pairs={{0,7},{1,6},{2,1},{3,0},{4,3},{5,2},{6,5},{7,4},{8,15},{9,14},{10,... | collective-permute-start | bytes 1769480 | tf_op jit(solution)/shard_map/ppermute | solution.py:434
  9.0 1.1 %copy-start = (bf16[2304,128]{1,0:T(8,128)(2,1)S(1)}, bf16[2304,128]{1,0:T(8,128)(2,1)}, u32[]{:S(2)}) copy-start(bf16[2304,128]{1,0:T(8,128)(2,1)} %get-tuple-element.17.q0.refs_0_.refs_4_.refs_8_) | copy-start | bytes 1769476
  68.9 9.8 %copy-start.1 = (bf16[2304,128]{1,0:T(8,128)(2,1)S(1)}, bf16[2304,128]{1,0:T(8,128)(2,1)}, u32[]{:S(2)}) copy-start(bf16[2304,128]{1,0:T(8,128)(2,1)} %get-tuple-element.17.q0.refs_0_.refs_4_.refs_8_) | copy-start | bytes 1769476
  70.1 19.9 %all-to-all-start.1 = ((bf16[8,144,128]{2,1,0:T(8,128)(2,1)}), bf16[8,144,128]{2,1,0:T(8,128)(2,1)S(1)}, u32[]{:S(2)}, u32[]{:S(2)}) async-start(bf16[8,144,128]{2,1,0:T(8,128)(2,1)} %fold.1), calls=%async_computation.1 | async-start | bytes 589824 | tf_op jit(solution)/shard_map/all_to_all | solution.py:442

commit v4 on v3

--- a/solution.py
+++ b/solution.py
@@ -186,43 +186,36 @@
 
     row, lane = eye_mask(64)
 
-    @pl.loop(0, 4)
-    def _(step):
-        head = step // 2
-        j = step % 2
-
-        for n, ref in enumerate((q0, q1)):
-
-            @pl.when(j == n)
-            def _():
-                q_s[...] = ref[pl.ds(pl.multiple_of(head * 1024, 1024), 1024), :]
-
-        for s in range(4):
-            q = q_s[s * SUB : (s + 1) * SUB, :]
-            peak = None
-            for b in range(2048 // KEY_BLOCK):
-                keys = slice(b * KEY_BLOCK, (b + 1) * KEY_BLOCK)
-                scores = dot_nt(q, k_ref[head, keys, :])
-                top = jnp.ceil(jnp.max(scores, axis=1, keepdims=True) * SCALE)
-                new = top if peak is None else jnp.maximum(peak, top)
-                weights = jnp.exp2(scores * SCALE - new).astype(BF)
-                part = dot_nn(weights, v_ref[head, keys, :])
-                acc = part if peak is None else acc * jnp.exp2(peak - new) + part
-                peak = new
-            unit = 2 * (place(j) + s // 2) + head
-            for d in range(4):
-                dest = 4 * (s % 2) + d
-                rows = slice(d * 64, (d + 1) * 64)
-                to = pl.ds(pl.multiple_of(unit * 64, 64), 64)
-                o_s[dest, to, :] = acc[rows, 0:128].astype(BF)
-                pair = jnp.where(
-                    lane == row,
-                    peak[rows, :],
-                    jnp.where(lane == row + 64, acc[rows, 128:256], 0.0),
-                )
-                st_s[dest, pl.ds(unit, 1), :] = jnp.sum(pair, axis=0, keepdims=True)
-        send(head, j, 0).start()
-        send(head, j, 1).start()
+    @pl.loop(0, 2)
+    def _(head):
+        for j in range(2):
+            for s in range(4):
+                rows = pl.ds(pl.multiple_of(head * 1024 + s * SUB, SUB), SUB)
+                q = (q0, q1)[j][rows, :]
+                peak = None
+                for b in range(2048 // KEY_BLOCK):
+                    keys = slice(b * KEY_BLOCK, (b + 1) * KEY_BLOCK)
+                    scores = dot_nt(q, k_ref[head, keys, :])
+                    top = jnp.ceil(jnp.max(scores, axis=1, keepdims=True) * SCALE)
+                    new = top if peak is None else jnp.maximum(peak, top)
+                    weights = jnp.exp2(scores * SCALE - new).astype(BF)
+                    part = dot_nn(weights, v_ref[head, keys, :])
+                    acc = part if peak is None else acc * jnp.exp2(peak - new) + part
+                    peak = new
+                unit = 2 * (place(j) + s // 2) + head
+                for d in range(4):
+                    dest = 4 * (s % 2) + d
+                    rows = slice(d * 64, (d + 1) * 64)
+                    to = pl.ds(pl.multiple_of(unit * 64, 64), 64)
+                    o_s[dest, to, :] = acc[rows, 0:128].astype(BF)
+                    pair = jnp.where(
+                        lane == row,
+                        peak[rows, :],
+                        jnp.where(lane == row + 64, acc[rows, 128:256], 0.0),
+                    )
+                    st_s[dest, pl.ds(unit, 1), :] = jnp.sum(pair, axis=0, keepdims=True)
+            send(head, j, 0).start()
+            send(head, j, 1).start()
 
     for dest in range(8):
         stats = st_s[dest]

time: 91.3 us -> 91.2 us (level)
  no operation moved by 1% of the time
where the time goes in v4:
time: 91.2 us; the launch traced here: 90.9 us
  blocking collectives  35.2 us (39%)
  Pallas kernels  31.7 us (35%)
  starting transfers between devices  10.9 us (12%)
  waiting for transfers between devices  10.5 us (12%)
  between operations  1.54 us (2%)
  local copies, waits for them, and re-layouts  1.07 us (1%)
    all_to_all x1, blocking collectives, swap(): lax.all_to_all(parts, 'context', split_axis=0, concat_axis=0, axis_index_...  35.2 us
    pallas_call x2, Pallas kernels, attend(): pl.pallas_call(functools.partial(attend_kernel, base=0 if before is None...  23.2 us
    all_to_all x1, waiting for transfers between devices, swap(): lax.all_to_all(parts, 'context', split_axis=0, concat_axis=0, axis_index_...  10.1 us
    all_to_all x1, starting transfers between devices, swap(): lax.all_to_all(parts, 'context', split_axis=0, concat_axis=0, axis_index_...  8.48 us
    pallas_call x1, Pallas kernels, turn(): pl.pallas_call(turn_kernel, in_specs=[pl.BlockSpec(memory_space=pltpu.SME...  3.92 us
  transfers between devices with their start and end apart: 4, of which 2 were waited for; matrix products, arithmetic and copies ran while one was open for 0% of the time, Pallas kernels for 15%

profile of v4, /device:TPU:8, one launch (start us, length us, event | category | flops | bytes accessed | tf_op | source)
XLA Modules:
  0.0 90.9 jit_solution(9901104230587540328)
XLA Ops:
  0.0 0.0 copy-start.3
  0.0 0.0 copy-start.2
  0.8 3.9 %turn.1 = (bf16[2304,128]{1,0:T(8,128)(2,1)}, bf16[2304,128]{1,0:T(8,128)(2,1)}, bf16[2304,128]{1,0:T(8,128)(2,1)}, bf16[2304,128]{1,0:T(8,128)(2,1)}) custom-call(s32[1]{0:T(128)S(6)} %copy.13.offset, s32[1,64]{1,0:T(1,128)} %bitcast.11, f32[1,128]{1,0:T(1,128)} %constant.32.clone.freq_ref, bf16[64,8,128]{2,1,0:T(8,128)(2,1)} %k_ref.1, ...), custom_call_target="tpu_custom_call" | custom-call | tf_op jit(solution)/shard_map/turn/pallas_call | solution.py:115
  4.7 0.1 collective-permute-start.2
  4.8 1.7 %collective-permute-start = (bf16[2304,128]{1,0:T(8,128)(2,1)}, bf16[2304,128]{1,0:T(8,128)(2,1)S(1)}, u32[]{:S(2)}, u32[]{:S(2)}) collective-permute-start(bf16[2304,128]{1,0:T(8,128)(2,1)} %get-tuple-element.13), channel_id=1, source_target_pairs={{0,2},{1,3},{2,4},{3,5},{4,6},{5,7},{6,0},{7,1},{8,10},{9,11},{10,... | collective-permute-start | bytes 1769480 | tf_op jit(solution)/shard_map/ppermute | solution.py:426
  6.5 0.6 collective-permute-start.1
  7.8 0.0 copy-done.3
  7.8 0.0 copy-done.2
  7.8 1.1 %lay.1 = (bf16[2,2048,128]{2,1,0:T(8,128)(2,1)S(1)}, bf16[2,2048,256]{2,1,0:T(8,128)(2,1)S(1)}) custom-call(s32[1]{0:T(128)S(6)} %copy.12.length, bf16[4096,128]{1,0:T(8,128)(2,1)S(1)} %bitcast.9, bf16[4096,128]{1,0:T(8,128)(2,1)S(1)} %bitcast.10), custom_call_target="tpu_custom_call" | custom-call | tf_op jit(solution)/shard_map/lay/pallas_call | solution.py:152
  8.9 0.0 collective-permute-done.2.q1.refs_1_.refs_5_.refs_9_
  9.0 0.0 copy-start
  9.0 1.1 %copy-done = bf16[2304,128]{1,0:T(8,128)(2,1)S(1)} copy-done((bf16[2304,128]{1,0:T(8,128)(2,1)S(1)}, bf16[2304,128]{1,0:T(8,128)(2,1)}, u32[]{:S(2)}) %copy-start) | copy-done | bytes 589848
  10.0 11.6 %near.1.refs_0_ = bf16[8,1056,128]{2,1,0:T(8,128)(2,1)S(1)} custom-call(bf16[2304,128]{1,0:T(8,128)(2,1)S(1)} %copy-done, bf16[2304,128]{1,0:T(8,128)(2,1)S(1)} %collective-permute-done.2.q1.refs_1_.refs_5_.refs_9_, bf16[2,2048,128]{2,1,0:T(8,128)(2,1)S(1)} %get-tuple-element.15.k_ref, bf16[2,2048,256]{2,1,0:T(8,128)(2,1)S(1)} %get-tuple-element.16.v_ref), custom_call_target="tpu_custom_call" | custom-call | flops 4294967296 | bytes 4194304 | tf_op jit(solution)/shard_map/near/pallas_call | solution.py:242
  21.6 0.0 collective-permute-done.q0.refs_2_.refs_6_.refs_10_
  21.6 0.4 collective-permute-done.1.q1.refs_3_.refs_7_.refs_11_
  22.0 11.6 %far.1 = bf16[8,1056,128]{2,1,0:T(8,128)(2,1)S(1)} custom-call(bf16[2304,128]{1,0:T(8,128)(2,1)S(1)} %collective-permute-done.q0.refs_2_.refs_6_.refs_10_, bf16[2304,128]{1,0:T(8,128)(2,1)S(1)} %collective-permute-done.1.q1.refs_3_.refs_7_.refs_11_, bf16[2,2048,128]{2,1,0:T(8,128)(2,1)S(1)} %get-tuple-element.15.k_ref, ...), custom_call_target="tpu_custom_call", output_to_operand_aliasing={{}: (4, {})} | custom-call | flops 4294967296 | bytes 4194304 | tf_op jit(solution)/shard_map/far/pallas_call | solution.py:242
  33.6 35.2 %all_to_all.10.in_ref = bf16[8,1056,128]{2,1,0:T(8,128)(2,1)S(1)} all-to-all(bf16[8,1056,128]{2,1,0:T(8,128)(2,1)S(1)} %far.1), channel_id=1, replica_groups={{0,4,8,12,16,20,24,28},{32,36,40,44,48,52,56,60},{64,68,72,76,80,84,88,..., dimensions={0} | all-to-all | bytes 4325376 | tf_op jit(solution)/shard_map/all_to_all | solution.py:435
  68.8 0.0 copy-start.1
  68.8 1.2 %fold.1 = bf16[8,144,128]{2,1,0:T(8,128)(2,1)} custom-call(bf16[8,1056,128]{2,1,0:T(8,128)(2,1)S(1)} %all_to_all.10.in_ref), custom_call_target="tpu_custom_call" | custom-call | tf_op jit(solution)/shard_map/fold/pallas_call | solution.py:319
  70.0 8.5 %all-to-all-start.1 = ((bf16[8,144,128]{2,1,0:T(8,128)(2,1)}), bf16[8,144,128]{2,1,0:T(8,128)(2,1)S(1)}, u32[]{:S(2)}, u32[]{:S(2)}) async-start(bf16[8,144,128]{2,1,0:T(8,128)(2,1)} %fold.1), calls=%async_computation.1 | async-start | bytes 589824 | tf_op jit(solution)/shard_map/all_to_all | solution.py:435
  78.5 0.1 pad_add_fusion.where
  78.5 0.1 pad_add_fusion.1.slots
  78.6 0.0 copy-done.1
  78.6 1.2 %prompt.1 = (bf16[2,64,128]{2,1,0:T(8,128)(2,1)S(1)}, f32[2,8,128]{2,1,0:T(8,128)S(1)}) custom-call(s32[2]{0:T(128)S(1)} %pad_add_fusion.where, s32[4]{0:T(128)S(1)} %pad_add_fusion.1.slots, bf16[2304,128]{1,0:T(8,128)(2,1)S(1)} %copy-done.1, bf16[2304,128]{1,0:T(8,128)(2,1)S(1)} %collective-permute-done.2.q1.refs_1_.refs_5_.refs_9_, ...), custom_call_target="tpu_custom_call" | custom-call | tf_op jit(solution)/shard_map/prompt/pallas_call | solution.py:362
  79.8 10.1 %all-to-all-done.1.got_ref = bf16[8,144,128]{2,1,0:T(8,128)(2,1)S(1)} async-done(((bf16[8,144,128]{2,1,0:T(8,128)(2,1)}), bf16[8,144,128]{2,1,0:T(8,128)(2,1)S(1)}, u32[]{:S(2)}, u32[]{:S(2)}) %all-to-all-start.1) | async-done | bytes 294944 | tf_op jit(solution)/shard_map/all_to_all | solution.py:435
  89.9 1.0 %final.1 = bf16[4,32,128]{2,1,0:T(8,128)(2,1)} custom-call(bf16[8,144,128]{2,1,0:T(8,128)(2,1)S(1)} %all-to-all-done.1.got_ref, bf16[2,64,128]{2,1,0:T(8,128)(2,1)S(1)} %get-tuple-element.19.po_ref, f32[2,8,128]{2,1,0:T(8,128)S(1)} %get-tuple-element.20.pst_ref), custom_call_target="tpu_custom_call" | custom-call | tf_op jit(solution)/shard_map/final/pallas_call | solution.py:405
Async XLA Ops:
  0.0 7.8 %copy-start.3 = (bf16[2048,2,128]{2,1,0:T(2,128)(2,1)S(1)}, bf16[2048,2,128]{2,1,0:T(2,128)(2,1)}, u32[]{:S(2)}) copy-start(bf16[2048,2,128]{2,1,0:T(2,128)(2,1)} %param.13) | copy-start | bytes 3145732
  0.0 7.8 %copy-start.2 = (bf16[2048,2,128]{2,1,0:T(2,128)(2,1)S(1)}, bf16[2048,2,128]{2,1,0:T(2,128)(2,1)}, u32[]{:S(2)}) copy-start(bf16[2048,2,128]{2,1,0:T(2,128)(2,1)} %param.12) | copy-start | bytes 3145732
  4.7 4.2 %collective-permute-start.2 = (bf16[2304,128]{1,0:T(8,128)(2,1)}, bf16[2304,128]{1,0:T(8,128)(2,1)S(1)}, u32[]{:S(2)}, u32[]{:S(2)}) collective-permute-start(bf16[2304,128]{1,0:T(8,128)(2,1)} %get-tuple-element.18), channel_id=1, source_target_pairs={{0,1},{1,0},{2,3},{3,2},{4,5},{5,4},{6,7},{7,6},{8,9},{9,8},{10,11... | collective-permute-start | bytes 1769480 | tf_op jit(solution)/shard_map/ppermute | solution.py:428
  4.8 16.8 %collective-permute-start = (bf16[2304,128]{1,0:T(8,128)(2,1)}, bf16[2304,128]{1,0:T(8,128)(2,1)S(1)}, u32[]{:S(2)}, u32[]{:S(2)}) collective-permute-start(bf16[2304,128]{1,0:T(8,128)(2,1)} %get-tuple-element.13), channel_id=1, source_target_pairs={{0,2},{1,3},{2,4},{3,5},{4,6},{5,7},{6,0},{7,1},{8,10},{9,11},{10,... | collective-permute-start | bytes 1769480 | tf_op jit(solution)/shard_map/ppermute | solution.py:426
  6.5 15.5 %collective-permute-start.1 = (bf16[2304,128]{1,0:T(8,128)(2,1)}, bf16[2304,128]{1,0:T(8,128)(2,1)S(1)}, u32[]{:S(2)}, u32[]{:S(2)}) collective-permute-start(bf16[2304,128]{1,0:T(8,128)(2,1)} %get-tuple-element.14), channel_id=1, source_target_pairs={{0,7},{1,6},{2,1},{3,0},{4,3},{5,2},{6,5},{7,4},{8,15},{9,14},{10,... | collective-permute-start | bytes 1769480 | tf_op jit(solution)/shard_map/ppermute | solution.py:427
  9.0 1.1 %copy-start = (bf16[2304,128]{1,0:T(8,128)(2,1)S(1)}, bf16[2304,128]{1,0:T(8,128)(2,1)}, u32[]{:S(2)}) copy-start(bf16[2304,128]{1,0:T(8,128)(2,1)} %get-tuple-element.17.q0.refs_0_.refs_4_.refs_8_) | copy-start | bytes 1769476
  68.8 9.8 %copy-start.1 = (bf16[2304,128]{1,0:T(8,128)(2,1)S(1)}, bf16[2304,128]{1,0:T(8,128)(2,1)}, u32[]{:S(2)}) copy-start(bf16[2304,128]{1,0:T(8,128)(2,1)} %get-tuple-element.17.q0.refs_0_.refs_4_.refs_8_) | copy-start | bytes 1769476
  70.0 19.9 %all-to-all-start.1 = ((bf16[8,144,128]{2,1,0:T(8,128)(2,1)}), bf16[8,144,128]{2,1,0:T(8,128)(2,1)S(1)}, u32[]{:S(2)}, u32[]{:S(2)}) async-start(bf16[8,144,128]{2,1,0:T(8,128)(2,1)} %fold.1), calls=%async_computation.1 | async-start | bytes 589824 | tf_op jit(solution)/shard_map/all_to_all | solution.py:435
